TPU v7x, 32 devices: a whole 2x2x4 slice. The times are simulated.
32 devices in a mesh: groups: 2 (over x), batch: 4 (over z), mp: 4 (over y, core).
Axes of the slice: x: 2, y: 2, z: 4, core: 2. Of those that a mesh axis runs over, the one named last changes fastest.
Arguments:
- queries: bfloat16 [32, 32, 4096], P(('groups', 'batch'), None, 'mp'), parts along dimension 0, may hold values from -8 to 8
- prefix_key_cache: bfloat16 [32, 4096, 512], P(('groups', 'batch'), 'mp'), parts along dimension 0, may hold values from -8 to 8
- prefix_value_cache: bfloat16 [32, 4096, 512], P(('groups', 'batch'), 'mp'), parts along dimension 0, may hold values from -6 to 6
- tree_node_keys: bfloat16 [32, 32, 512], P(('groups', 'batch')), parts along dimension 0, may hold values from -8 to 8
- tree_node_values: bfloat16 [32, 32, 512], P(('groups', 'batch')), parts along dimension 0, may hold values from -6 to 6
- lengths: int32 [32], P(('groups', 'batch')), parts along dimension 0, may hold values from 1024 to 4096, as said below
- parents: int32 [32, 32], P(('groups', 'batch')), parts along dimension 0, may hold values from 0 to 30, as said below
- request_adapter_index: int32 [32], P('groups'), parts along dimension 0, may hold values from 0 to 15, as said below
- output_projection_weight: bfloat16 [4096, 8192], P('mp'), may hold values from -0.23925781 to 0.23925781
- adapter_down_weight: bfloat16 [16, 64, 4096], P('batch', None, 'mp'), may hold values from -0.09375 to 0.09375
- adapter_up_weight: bfloat16 [16, 64, 8192], P('batch', None, 'mp'), may hold values from -0.75 to 0.75
Outputs:
- block_output: bfloat16 [32, 32, 8192], P(('groups', 'batch'), None, 'mp'), parts along dimension 0
There are 2 independent parts, one for each index of `groups`. A program takes and returns all parts, laid end to end along the dimension named above; an argument that names none is the same for every part. Nothing has to cross between parts.
Inputs may be any that keep to these rules, and one draw needn't show every extreme that they name: `lengths`: at least 2; one request of every draw has a prefix of exactly 4096. parents[r, 0] = 0 and parents[r, i] < i for i >= 1. `request_adapter_index`: adapter a is held by batch index a // 4; among the 4 requests of one batch index (requests b * 4 to b * 4 + 3) at most 2 use adapters held by one batch index, and in every such block one batch index serves exactly 2.
All inputs are finite; a program needn't handle non-finite values.
Results may differ from a plain program's by a relative error of at most 0.022.
Values may be sent and summed in bfloat16 or wider, within the bound.
A program may use at most 128 MiB of HBM per device.

v0:
```python
import math

import jax
import jax.numpy as jnp
from jax import lax
from jax.sharding import PartitionSpec as P

HEAD_WIDTH = 128
ADAPTER_RANK = 64
CAP = 2


NEG_FILL = -1e30
ADAPTER_SCALE = 2.0


def ancestors(parents):
    tree_node_count = parents.shape[-1]
    identity_mat = jnp.eye(tree_node_count, dtype=jnp.float32)
    parent_mat = (
        parents[..., :, None] == jnp.arange(tree_node_count, dtype=jnp.int32)[None, :]
    ).astype(jnp.float32)
    reached = jnp.minimum(identity_mat + parent_mat, 1.0)
    for repeat in range(max(1, (tree_node_count - 1).bit_length())):
        reached = jnp.minimum(jnp.matmul(reached, reached, precision=lax.Precision.HIGHEST), 1.0)
    return reached > 0.5


def per_device(
    queries,
    prefix_key_cache,
    prefix_value_cache,
    tree_node_keys,
    tree_node_values,
    lengths,
    parents,
    request_adapter_index,
    output_projection_weight,
    adapter_down_weight,
    adapter_up_weight,
):
    request_count, tree_node_count, width_here = queries.shape
    heads_here = width_here // HEAD_WIDTH
    head_total = heads_here * lax.axis_size("mp")
    prefix_here = prefix_key_cache.shape[1]
    kv_heads = prefix_key_cache.shape[2] // HEAD_WIDTH
    group_size = head_total // kv_heads
    inv_root = 1.0 / math.sqrt(HEAD_WIDTH)
    column = lax.axis_index("mp")
    every_query = lax.all_gather(queries, "mp", axis=2, tiled=True)
    query_blocks = every_query.reshape(
        request_count, tree_node_count, kv_heads, group_size, HEAD_WIDTH
    )
    key_blocks = prefix_key_cache.reshape(request_count, prefix_here, kv_heads, HEAD_WIDTH)
    value_blocks = prefix_value_cache.reshape(request_count, prefix_here, kv_heads, HEAD_WIDTH)
    scores = (
        jnp.einsum(
            "rngid,rpgd->rngip", query_blocks, key_blocks, preferred_element_type=jnp.float32
        )
        * inv_root
    )
    places = column * prefix_here + jnp.arange(prefix_here, dtype=jnp.int32)
    valid = (places[None, :] < lengths[:, None])[:, None, None, None, :]
    local_top = jnp.max(jnp.where(valid, scores, NEG_FILL), axis=-1)
    weights = jnp.where(valid, jnp.exp(scores - local_top[..., None]), 0.0)
    totals = jnp.sum(weights, axis=-1).reshape(request_count, tree_node_count, head_total)
    summed = jnp.einsum(
        "rngip,rpgd->rngid",
        weights.astype(jnp.bfloat16),
        value_blocks,
        preferred_element_type=jnp.float32,
    )
    summed = summed.reshape(request_count, tree_node_count, head_total, HEAD_WIDTH)
    tops = local_top.reshape(request_count, tree_node_count, head_total)
    got_acc, got_top, got_sum = (
        lax.all_to_all(
            summed[None].astype(jnp.bfloat16), "mp", split_axis=3, concat_axis=0, tiled=True
        ).astype(jnp.float32),
        lax.all_to_all(
            tops[None].astype(jnp.bfloat16), "mp", split_axis=3, concat_axis=0, tiled=True
        ).astype(jnp.float32),
        lax.all_to_all(
            totals[None].astype(jnp.bfloat16), "mp", split_axis=3, concat_axis=0, tiled=True
        ).astype(jnp.float32),
    )
    prefix_top = jnp.max(got_top, axis=0)
    factor = jnp.exp(got_top - prefix_top[None])
    prefix_acc = jnp.sum(got_acc * factor[..., None], axis=0)
    prefix_sum = jnp.sum(got_sum * factor, axis=0)
    kv_group = column * heads_here // group_size
    tree_k = lax.dynamic_slice_in_dim(tree_node_keys, kv_group * HEAD_WIDTH, HEAD_WIDTH, 2)
    tree_v = lax.dynamic_slice_in_dim(tree_node_values, kv_group * HEAD_WIDTH, HEAD_WIDTH, 2)
    own_q = queries.reshape(request_count, tree_node_count, heads_here, HEAD_WIDTH)
    tree_scores = (
        jnp.einsum("rnid,rmd->rnim", own_q, tree_k, preferred_element_type=jnp.float32) * inv_root
    )
    linked = ancestors(parents)[:, :, None, :]
    tree_top = jnp.max(jnp.where(linked, tree_scores, NEG_FILL), axis=-1)
    top_value = jnp.maximum(prefix_top, tree_top)
    tree_w = jnp.where(linked, jnp.exp(tree_scores - top_value[..., None]), 0.0)
    lift_up = jnp.exp(prefix_top - top_value)
    numerator = prefix_acc * lift_up[..., None] + jnp.einsum(
        "rnim,rmd->rnid", tree_w.astype(jnp.bfloat16), tree_v, preferred_element_type=jnp.float32
    )
    denominator = prefix_sum * lift_up + jnp.sum(tree_w, axis=-1)
    attended = (
        (numerator / denominator[..., None])
        .astype(jnp.bfloat16)
        .reshape(request_count, tree_node_count, width_here)
    )
    batch_size = lax.axis_size("batch")
    batch_row = lax.axis_index("batch")
    adapters_present = adapter_down_weight.shape[0]
    mine_ids = lax.dynamic_slice_in_dim(
        request_adapter_index, batch_row * request_count, request_count
    )
    every_ids = request_adapter_index.reshape(batch_size, request_count)
    owner_all = every_ids // adapters_present
    is_mine = (owner_all == batch_row).astype(jnp.int32)
    slot_rank = jnp.cumsum(is_mine, axis=1) - is_mine
    slot_ids = jnp.arange(CAP, dtype=jnp.int32)
    select = (
        (slot_rank[:, None, :] == slot_ids[None, :, None]) & (is_mine[:, None, :] == 1)
    ).astype(jnp.bfloat16)
    which_local = (
        (every_ids % adapters_present)[:, :, None]
        == jnp.arange(adapters_present, dtype=jnp.int32)[None, None, :]
    ).astype(jnp.bfloat16)
    picked = jnp.einsum(
        "dcr,dra->dca", select, which_local, preferred_element_type=jnp.float32
    ).astype(jnp.bfloat16)
    send_down = jnp.einsum(
        "dca,ax->dcx",
        picked,
        adapter_down_weight.reshape(adapters_present, -1),
        preferred_element_type=jnp.float32,
    ).astype(jnp.bfloat16)
    send_up = jnp.einsum(
        "dca,ax->dcx",
        picked,
        adapter_up_weight.reshape(adapters_present, -1),
        preferred_element_type=jnp.float32,
    ).astype(jnp.bfloat16)
    got_down, got_up = (
        lax.all_to_all(send_down, "batch", split_axis=0, concat_axis=0, tiled=True),
        lax.all_to_all(send_up, "batch", split_axis=0, concat_axis=0, tiled=True),
    )
    my_owner = mine_ids // adapters_present
    positions = jnp.arange(request_count, dtype=jnp.int32)
    earlier = (my_owner[:, None] == my_owner[None, :]) & (positions[None, :] < positions[:, None])
    my_rank = jnp.sum(earlier.astype(jnp.int32), axis=1)
    slot_code = my_owner * CAP + my_rank
    choose = (slot_code[:, None] == jnp.arange(batch_size * CAP, dtype=jnp.int32)[None, :]).astype(
        jnp.bfloat16
    )
    source_down = got_down.reshape(batch_size * CAP, -1)
    source_up = got_up.reshape(batch_size * CAP, -1)
    down_req = (
        jnp.dot(choose, source_down, preferred_element_type=jnp.float32)
        .astype(jnp.bfloat16)
        .reshape(request_count, ADAPTER_RANK, width_here)
    )
    up_req = (
        jnp.dot(choose, source_up, preferred_element_type=jnp.float32)
        .astype(jnp.bfloat16)
        .reshape(request_count, ADAPTER_RANK, -1)
    )
    flat_rows = attended.reshape(request_count * tree_node_count, width_here)
    partial_value = jnp.dot(flat_rows, output_projection_weight, preferred_element_type=jnp.float32)
    projected_output = lax.psum_scatter(
        partial_value.astype(jnp.bfloat16), "mp", scatter_dimension=1, tiled=True
    ).astype(jnp.float32)
    shrink_part = jnp.einsum("rnh,rkh->rnk", attended, down_req, preferred_element_type=jnp.float32)
    shrunk = lax.psum(shrink_part.astype(jnp.bfloat16), "mp")
    raised_output = jnp.einsum("rnk,rkd->rnd", shrunk, up_req, preferred_element_type=jnp.float32)
    return (
        projected_output.reshape(request_count, tree_node_count, -1) + ADAPTER_SCALE * raised_output
    ).astype(jnp.bfloat16)


def solution(mesh):
    return jax.shard_map(
        per_device,
        mesh=mesh,
        in_specs=(
            P(("groups", "batch"), None, "mp"),
            P(("groups", "batch"), "mp", None),
            P(("groups", "batch"), "mp", None),
            P(("groups", "batch"), None, None),
            P(("groups", "batch"), None, None),
            P(("groups", "batch")),
            P(("groups", "batch"), None),
            P("groups"),
            P("mp", None),
            P("batch", None, "mp"),
            P("batch", None, "mp"),
        ),
        out_specs=P(("groups", "batch"), None, "mp"),
        check_vma=False,
    )
```

profile of v0, /device:TPU:0, one launch (start us, length us, event | category | flops | bytes accessed | tf_op | source)
XLA Modules:
  0.0 185.0 jit_solution(17431741187601200361)
XLA Ops:
  6.5 0.7 all-gather.2.cloned.1.call-update
  7.3 1.0 convolution_minimum_fusion.4
  8.3 0.2 convolution_minimum_fusion.3
  8.5 0.2 convolution_minimum_fusion.2
  8.7 0.2 convolution_minimum_fusion.1
  8.9 0.2 fusion.25
  9.2 6.9 %reshape.262 = bf16[4,1024,4,128]{3,2,1,0:T(4,128)(2,1)} reshape(bf16[4,1024,512]{2,1,0:T(8,128)(2,1)} %param.12) | data formatting | bytes 8388608 | tf_op jit(solution)/shard_map/reshape | solution.py:54
  16.2 7.0 %reshape.264 = bf16[4,1024,4,128]{3,2,1,0:T(4,128)(2,1)} reshape(bf16[4,1024,512]{2,1,0:T(8,128)(2,1)} %param.13) | data formatting | bytes 8388608 | tf_op jit(solution)/shard_map/reshape | solution.py:55
  23.2 0.4 reshape.287
  23.7 0.2 reduce_window_sum.11
  23.9 0.2 convolution_convert_fusion.6
  24.1 0.5 convolution_convert_fusion.2
  24.6 2.1 %copy.109 = bf16[4,2,65536]{2,1,0:T(2,128)(2,1)} copy(bf16[4,2,65536]{2,0,1:T(4,128)(2,1)S(1)} %convolution_convert_fusion.2) | data formatting | bytes 2097152 | tf_op jit(solution)/shard_map/convert_element_type | solution.py:137
  26.8 1.3 select_reduce_fusion
  28.1 0.3 all-gather.2.cloned.1.call-done
  28.4 1.5 copy.123
  29.8 10.9 %fusion = (f32[4,32,4,8]{1,3,2,0:T(8,128)S(1)}, f32[4,4,1024,32,8]{2,3,4,1,0:T(8,128)}) fusion(pred[4,1024]{1,0:T(4,128)(4,1)S(1)} %broadcast_compare_fusion, bf16[4,32,4,8,128]{4,3,2,1,0:T(8,128)(2,1)S(1)} %bitcast.125, bf16[4,1024,4,128,1]{3,2,1,0,4:T(4,128)(2,1)} %bitcast.119), kind=kOutput, calls=%fused_computation.6 | convolution fusion | flops 1086320640 | bytes 22040576 | tf_op jit(solution)/shard_map/rngid,rpgd->rngip/dot_general | solution.py:57
  40.8 0.7 reshape.291
  41.5 4.0 %all-to-all-start.1 = ((bf16[4,2,512]{2,1,0:T(2,128)(2,1)}), bf16[4,2,512]{2,1,0:T(2,128)(2,1)S(1)}, u32[]{:S(2)}, u32[]{:S(2)}) async-start(bf16[4,2,512]{2,1,0:T(2,128)(2,1)} %reshape.291), calls=%async_computation.1 | async-start | bytes 16384 | tf_op jit(solution)/shard_map/all_to_all | solution.py:79
  45.5 9.4 %fusion.17 = bf16[4,4,32,8,128]{4,2,3,1,0:T(8,128)(2,1)S(1)} fusion(bf16[4,1024,4,128,1]{3,2,1,0,4:T(4,128)(2,1)} %bitcast.118, f32[4,4,1024,32,8]{2,3,4,1,0:T(8,128)} %get-tuple-element.16, f32[4,32,4,8]{1,3,2,0:T(8,128)S(1)} %get-tuple-element.15, pred[4,1024]{1,0:T(4,128)(4,1)S(1)} %broadcast_compare_fusion), kind=kOutput, calls=%fused_computation.25 | convolution fusion | flops 1091043328 | bytes 22040576 | tf_op jit(solution)/shard_map/rngip,rpgd->rngid/dot_general | solution.py:67
  55.0 2.3 %copy-done.1 = f32[4,4,1024,32,8]{2,3,4,1,0:T(8,128)S(1)} copy-done((f32[4,4,1024,32,8]{2,3,4,1,0:T(8,128)S(1)}, f32[4,4,1024,32,8]{2,3,4,1,0:T(8,128)}, u32[]{:S(2)}) %copy-start.1) | copy-done | bytes 16777240
  57.3 4.2 %fusion.3 = bf16[4,32,4,8]{1,3,2,0:T(8,128)(2,1)S(1)} fusion(f32[4,4,1024,32,8]{2,3,4,1,0:T(8,128)S(1)} %copy-done.1, f32[4,32,4,8]{1,3,2,0:T(8,128)S(1)} %get-tuple-element.15, pred[4,1024]{1,0:T(4,128)(4,1)S(1)} %broadcast_compare_fusion), kind=kLoop, calls=%fused_computation.9 | loop fusion | flops 16773120 | bytes 16805888 | tf_op jit(solution)/shard_map/reduce_sum | solution.py:66
  61.5 1.1 copy.96
  62.7 0.7 reshape.293
  63.4 3.3 %all-to-all-start.2 = ((bf16[4,2,512]{2,1,0:T(2,128)(2,1)}), bf16[4,2,512]{2,1,0:T(2,128)(2,1)S(1)}, u32[]{:S(2)}, u32[]{:S(2)}) async-start(bf16[4,2,512]{2,1,0:T(2,128)(2,1)} %reshape.293), calls=%async_computation.2 | async-start | bytes 16384 | tf_op jit(solution)/shard_map/all_to_all | solution.py:82
  66.8 3.7 %all-to-all-done.2 = bf16[4,2,512]{2,1,0:T(2,128)(2,1)S(1)} async-done(((bf16[4,2,512]{2,1,0:T(2,128)(2,1)}), bf16[4,2,512]{2,1,0:T(2,128)(2,1)S(1)}, u32[]{:S(2)}, u32[]{:S(2)}) %all-to-all-start.2) | async-done | bytes 8224 | tf_op jit(solution)/shard_map/all_to_all | solution.py:82
  70.5 3.5 %all-to-all-start = ((bf16[1,4,32,32,128]{4,2,1,0,3:T(8,128)(2,1)}), bf16[1,4,32,32,128]{4,2,1,0,3:T(8,128)(2,1)S(1)}, u32[]{:S(2)}, u32[]{:S(2)}) async-start(bf16[1,4,32,32,128]{4,2,1,0,3:T(8,128)(2,1)} %copy.96), calls=%async_computation | async-start | bytes 2097152 | tf_op jit(solution)/shard_map/all_to_all | solution.py:76
  74.0 0.2 fusion.31
  74.2 0.9 copy.104
  75.4 13.0 %all-to-all-done = bf16[1,4,32,32,128]{4,2,1,0,3:T(8,128)(2,1)S(1)} async-done(((bf16[1,4,32,32,128]{4,2,1,0,3:T(8,128)(2,1)}), bf16[1,4,32,32,128]{4,2,1,0,3:T(8,128)(2,1)S(1)}, u32[]{:S(2)}, u32[]{:S(2)}) %all-to-all-start) | async-done | bytes 1048608 | tf_op jit(solution)/shard_map/all_to_all | solution.py:76
  88.4 5.3 %all-to-all-start.3 = ((bf16[4,2,65536]{2,1,0:T(2,128)(2,1)}), bf16[4,2,65536]{2,1,0:T(2,128)(2,1)S(1)}, u32[]{:S(2)}, u32[]{:S(2)}) async-start(bf16[4,2,65536]{2,1,0:T(2,128)(2,1)} %copy.109), calls=%async_computation.4 | async-start | bytes 2097152 | tf_op jit(solution)/shard_map/all_to_all | solution.py:145
  93.7 0.7 fusion.16
  94.5 1.4 fusion.24
  95.9 9.6 %convolution_convert_fusion.4 = bf16[128,8192]{1,0:T(8,128)(2,1)} fusion(bf16[1024,8192]{1,0:T(8,128)(2,1)} %param.19, bf16[16,8,8,128]{3,2,1,0:T(8,128)(2,1)S(1)} %bitcast.122), kind=kOutput, calls=%fused_computation.11 | convolution fusion | flops 2148532224 | bytes 19136512 | tf_op jit(solution)/shard_map/dot_general | solution.py:169
  105.5 0.8 reshape.288
  106.3 0.9 convolution_convert_fusion
  107.1 3.5 %copy.111 = bf16[4,2,131072]{2,1,0:T(2,128)(2,1)} copy(bf16[4,2,131072]{2,0,1:T(4,128)(2,1)S(1)} %convolution_convert_fusion) | data formatting | bytes 4194304 | tf_op jit(solution)/shard_map/convert_element_type | solution.py:143
  110.6 8.6 %all-to-all-done.3 = bf16[4,2,65536]{2,1,0:T(2,128)(2,1)S(1)} async-done(((bf16[4,2,65536]{2,1,0:T(2,128)(2,1)}), bf16[4,2,65536]{2,1,0:T(2,128)(2,1)S(1)}, u32[]{:S(2)}, u32[]{:S(2)}) %all-to-all-start.3) | async-done | bytes 1048608 | tf_op jit(solution)/shard_map/all_to_all | solution.py:145
  119.2 3.6 %all-to-all-start.4 = ((bf16[4,2,131072]{2,1,0:T(2,128)(2,1)}), bf16[4,2,131072]{2,1,0:T(2,128)(2,1)S(1)}, u32[]{:S(2)}, u32[]{:S(2)}) async-start(bf16[4,2,131072]{2,1,0:T(2,128)(2,1)} %copy.111), calls=%async_computation.5 | async-start | bytes 4194304 | tf_op jit(solution)/shard_map/all_to_all | solution.py:146
  122.9 0.2 convert_reduce_fusion
  123.2 1.4 reshape.271
  124.6 1.7 convolution_convert_fusion.3
  126.4 0.3 convolution_convert_fusion.5
  126.7 11.5 %psum.7 = bf16[4,32,64]{2,1,0:T(8,128)(2,1)S(1)} all-reduce(bf16[4,32,64]{2,1,0:T(8,128)(2,1)S(1)} %convolution_convert_fusion.5), channel_id=1, replica_groups=mesh['groups'=2,'batch'=4,'mp'=4] {'mp'}, use_global_device_ids=true, to_apply=%region_10.11 | all-reduce | flops 8192 | bytes 32768 | tf_op jit(solution)/shard_map/psum | solution.py:174
  138.3 32.2 %all-to-all-done.4 = bf16[4,2,131072]{2,1,0:T(2,128)(2,1)S(1)} async-done(((bf16[4,2,131072]{2,1,0:T(2,128)(2,1)}), bf16[4,2,131072]{2,1,0:T(2,128)(2,1)S(1)}, u32[]{:S(2)}, u32[]{:S(2)}) %all-to-all-start.4) | async-done | bytes 2097184 | tf_op jit(solution)/shard_map/all_to_all | solution.py:146
  170.5 2.1 %reshape.274 = bf16[8,131072]{1,0:T(8,128)(2,1)} reshape(bf16[4,2,131072]{2,1,0:T(2,128)(2,1)S(1)} %all-to-all-done.4) | data formatting | bytes 4194304 | tf_op jit(solution)/shard_map/reshape | solution.py:157
  172.6 2.3 %convolution_convert_fusion.1 = bf16[4,131072]{1,0:T(4,128)(2,1)S(1)} fusion(bf16[8,131072]{1,0:T(8,128)(2,1)} %reshape.274, s32[4]{0:T(128)S(1)} %multiply_add_fusion.1), kind=kOutput, calls=%fused_computation.1 | convolution fusion | flops 8912928 | bytes 3145744 | tf_op jit(solution)/shard_map/dot_general | solution.py:164
  175.0 3.2 %fusion.15 = bf16[4,32,2048]{2,1,0:T(8,128)(2,1)} fusion(bf16[4,32,64]{2,1,0:T(8,128)(2,1)S(1)} %psum.7, bf16[1,4,64,2048]{3,1,2,0:T(4,128)(2,1)S(1)} %bitcast.121, bf16[4,32,2048]{2,1,0:T(8,128)(2,1)} %bitcast.127), kind=kOutput, calls=%fused_computation.22 | convolution fusion | flops 34603008 | bytes 2113536 | tf_op jit(solution)/shard_map/rnk,rkd->rnd/dot_general | solution.py:175
  (42 shorter events, 1.1 us)
Async XLA Ops:
  6.5 87.9 %copy-start = (bf16[4,32,512]{2,1,0:T(8,128)(2,1)S(1)}, bf16[4,32,512]{2,1,0:T(8,128)(2,1)}, u32[]{:S(2)}) copy-start(bf16[4,32,512]{2,1,0:T(8,128)(2,1)} %param.15) | copy-start | bytes 393220
  6.5 21.8 %all-gather.2.cloned.1.call-start = ((), (), s32[]{:S(2)}) async-start(), calls=%async_computation.6 | async-start | bytes 1310720 | tf_op jit(solution)/shard_map/all_gather | solution.py:50
  16.2 7.0 %copy-start.4 = (bf16[4,64,1024]{2,1,0:T(8,128)(2,1)S(1)}, bf16[4,64,1024]{2,1,0:T(8,128)(2,1)}, u32[]{:S(2)}) copy-start(bf16[4,64,1024]{2,1,0:T(8,128)(2,1)} %param.20) | copy-start | bytes 1572868
  16.2 7.4 %copy-start.5 = (s32[16]{0:T(128)S(1)}, s32[16]{0:T(128)}, u32[]{:S(2)}) copy-start(s32[16]{0:T(128)} %param.18) | copy-start | bytes 196
  23.2 3.5 %copy-start.6 = (s32[4]{0:T(128)S(1)}, s32[4]{0:T(128)}, u32[]{:S(2)}) copy-start(s32[4]{0:T(128)} %param.16) | copy-start | bytes 52
  23.2 3.6 %copy-start.2 = (bf16[4,32,1024]{2,1,0:T(8,128)(2,1)S(1)}, bf16[4,32,1024]{2,1,0:T(8,128)(2,1)}, u32[]{:S(2)}) copy-start(bf16[4,32,1024]{2,1,0:T(8,128)(2,1)} %param.11) | copy-start | bytes 786436
  41.5 21.9 %all-to-all-start.1 = ((bf16[4,2,512]{2,1,0:T(2,128)(2,1)}), bf16[4,2,512]{2,1,0:T(2,128)(2,1)S(1)}, u32[]{:S(2)}, u32[]{:S(2)}) async-start(bf16[4,2,512]{2,1,0:T(2,128)(2,1)} %reshape.291), calls=%async_computation.1 | async-start | bytes 16384 | tf_op jit(solution)/shard_map/all_to_all | solution.py:79
  45.5 11.8 %copy-start.1 = (f32[4,4,1024,32,8]{2,3,4,1,0:T(8,128)S(1)}, f32[4,4,1024,32,8]{2,3,4,1,0:T(8,128)}, u32[]{:S(2)}) copy-start(f32[4,4,1024,32,8]{2,3,4,1,0:T(8,128)} %get-tuple-element.16) | copy-start | bytes 50331652
  63.4 7.1 %all-to-all-start.2 = ((bf16[4,2,512]{2,1,0:T(2,128)(2,1)}), bf16[4,2,512]{2,1,0:T(2,128)(2,1)S(1)}, u32[]{:S(2)}, u32[]{:S(2)}) async-start(bf16[4,2,512]{2,1,0:T(2,128)(2,1)} %reshape.293), calls=%async_computation.2 | async-start | bytes 16384 | tf_op jit(solution)/shard_map/all_to_all | solution.py:82
  70.5 18.0 %all-to-all-start = ((bf16[1,4,32,32,128]{4,2,1,0,3:T(8,128)(2,1)}), bf16[1,4,32,32,128]{4,2,1,0,3:T(8,128)(2,1)S(1)}, u32[]{:S(2)}, u32[]{:S(2)}) async-start(bf16[1,4,32,32,128]{4,2,1,0,3:T(8,128)(2,1)} %copy.96), calls=%async_computation | async-start | bytes 2097152 | tf_op jit(solution)/shard_map/all_to_all | solution.py:76
  88.4 30.8 %all-to-all-start.3 = ((bf16[4,2,65536]{2,1,0:T(2,128)(2,1)}), bf16[4,2,65536]{2,1,0:T(2,128)(2,1)S(1)}, u32[]{:S(2)}, u32[]{:S(2)}) async-start(bf16[4,2,65536]{2,1,0:T(2,128)(2,1)} %copy.109), calls=%async_computation.4 | async-start | bytes 2097152 | tf_op jit(solution)/shard_map/all_to_all | solution.py:145
  93.7 81.3 %reduce-scatter.2.cloned.1.call-start = ((), (), s32[]{:S(2)}) async-start(), calls=%async_computation.7 | async-start | bytes 2621440 | tf_op jit(solution)/shard_map/reduce_scatter | solution.py:170
  95.9 9.6 %copy-start.3 = (bf16[4,64,2048]{2,1,0:T(8,128)(2,1)S(1)}, bf16[4,64,2048]{2,1,0:T(8,128)(2,1)}, u32[]{:S(2)}) copy-start(bf16[4,64,2048]{2,1,0:T(8,128)(2,1)} %param.21) | copy-start | bytes 3145732
  119.2 51.3 %all-to-all-start.4 = ((bf16[4,2,131072]{2,1,0:T(2,128)(2,1)}), bf16[4,2,131072]{2,1,0:T(2,128)(2,1)S(1)}, u32[]{:S(2)}, u32[]{:S(2)}) async-start(bf16[4,2,131072]{2,1,0:T(2,128)(2,1)} %copy.111), calls=%async_computation.5 | async-start | bytes 4194304 | tf_op jit(solution)/shard_map/all_to_all | solution.py:146
Sparse Core Ops, SparseCore 0:
  8.9 19.4 all-gather.1
  105.6 32.3 reduce-scatter.1
where the time goes:
time: 186 us; the launch traced here: 185 us
  waiting for transfers between devices  58.6 us (32%)
  matrix products  43.5 us (23%)
  local copies, waits for them, and re-layouts  32.1 us (17%)
  starting transfers between devices  19.7 us (11%)
  between operations  13.7 us (7%)
  blocking collectives  11.5 us (6%)
  other arithmetic  5.87 us (3%)
    all_to_all x1, waiting for transfers between devices, per_device(): lax.all_to_all(send_up, 'batch', split_axis=0, concat_axis=0, tiled=True)  32.2 us
    all_to_all x1, waiting for transfers between devices, per_device(): lax.all_to_all(summed[None].astype(jnp.bfloat16), 'mp', split_axis=3, con...  13 us
    psum x1, blocking collectives, per_device(): shrunk = lax.psum(shrink_part.astype(jnp.bfloat16), 'mp')  11.5 us
    dot_general x1, matrix products, per_device(): jnp.einsum('rngid,rpgd->rngip', query_blocks, key_blocks, preferred_eleme...  10.9 us
    dot_general x1, matrix products, per_device(): jnp.dot(flat_rows, output_projection_weight, preferred_element_type=jnp.f...  9.57 us
    dot_general x1, matrix products, per_device(): jnp.einsum('rngip,rpgd->rngid', weights.astype(jnp.bfloat16), value_block...  9.45 us
    all_to_all x1, waiting for transfers between devices, per_device(): lax.all_to_all(send_down, 'batch', split_axis=0, concat_axis=0, tiled=True)  8.63 us
    reshape x1, local copies, waits for them, and re-layouts, per_device(): prefix_value_cache.reshape(request_count, prefix_here, kv_heads, HEAD_WIDTH)  7.01 us
  transfers between devices with their start and end apart: 7, of which 5 were waited for; matrix products, arithmetic and copies ran while one was open for 34% of the time, Pallas kernels for 0%

commit v1 on v0

v1 whole, which is shorter than its diff:
```python
import functools
import math

import jax
import jax.numpy as jnp
from jax import lax
from jax.experimental import pallas as pl
from jax.experimental.pallas import tpu as pltpu
from jax.sharding import PartitionSpec as P

HEAD_WIDTH = 128
ADAPTER_RANK = 64
CAP = 2
LANES = 128
NEG_FILL = -1e30
ADAPTER_SCALE = 2.0
INV_ROOT = 1.0 / math.sqrt(HEAD_WIDTH)
VMEM_LIMIT = 48 << 20
CONTRACT_LAST = (((1,), (1,)), ((), ()))
CONTRACT_INNER = (((1,), (0,)), ((), ()))


def dot(a, b, dims=CONTRACT_INNER):
    return lax.dot_general(a, b, dims, preferred_element_type=jnp.float32)


def params(**more):
    return pltpu.CompilerParams(vmem_limit_bytes=VMEM_LIMIT, **more)


def ancestors(parents):
    tree_node_count = parents.shape[-1]
    identity_mat = jnp.eye(tree_node_count, dtype=jnp.float32)
    parent_mat = (
        parents[..., :, None] == jnp.arange(tree_node_count, dtype=jnp.int32)[None, :]
    ).astype(jnp.float32)
    reached = jnp.minimum(identity_mat + parent_mat, 1.0)
    for repeat in range(max(1, (tree_node_count - 1).bit_length())):
        step = reached.astype(jnp.bfloat16)
        reached = jnp.minimum(
            jnp.einsum("rnm,rmk->rnk", step, step, preferred_element_type=jnp.float32), 1.0
        )
    return reached


def pick_kernel(picked_ref, down_ref, up_ref, down_out, up_out):
    down_out[...] = down_ref[...]
    up_out[...] = up_ref[...]


def pick(picked, down, up):
    slots = picked.shape[0]
    present, rank, width = down.shape
    up_width = up.shape[2]
    return pl.pallas_call(
        pick_kernel,
        grid_spec=pltpu.PrefetchScalarGridSpec(
            num_scalar_prefetch=1,
            grid=(slots,),
            in_specs=[
                pl.BlockSpec((1, rank, width), lambda s, p: (p[s], 0, 0)),
                pl.BlockSpec((1, rank, up_width), lambda s, p: (p[s], 0, 0)),
            ],
            out_specs=[
                pl.BlockSpec((1, rank, width), lambda s, p: (s, 0, 0)),
                pl.BlockSpec((1, rank, up_width), lambda s, p: (s, 0, 0)),
            ],
        ),
        out_shape=[
            jax.ShapeDtypeStruct((slots, rank, width), down.dtype),
            jax.ShapeDtypeStruct((slots, rank, up_width), up.dtype),
        ],
        compiler_params=params(),
        name="pick",
    )(picked, down, up)


def attend_kernel(group_size, meta_ref, q_ref, k_ref, v_ref, out_ref):
    blocks, _, nodes, width_here = q_ref.shape
    heads_here = width_here // HEAD_WIDTH
    request = pl.program_id(0)
    positions = k_ref.shape[1]
    left = meta_ref[request]
    rows = []
    for block in range(blocks):
        for head in range(heads_here):
            rows.append(q_ref[block, 0, :, head * HEAD_WIDTH : (head + 1) * HEAD_WIDTH])
    query = jnp.concatenate(rows, axis=0)
    scores = dot(query, k_ref[0], CONTRACT_LAST) * INV_ROOT
    place = lax.broadcasted_iota(jnp.int32, (1, positions), 1)
    valid = place < left
    scores = jnp.where(valid, scores, NEG_FILL)
    top = jnp.max(scores, axis=1, keepdims=True).astype(jnp.bfloat16).astype(jnp.float32)
    weights = jnp.where(valid, jnp.exp(scores - top), 0.0)
    total = jnp.sum(weights, axis=1, keepdims=True)
    summed = dot(weights.astype(jnp.bfloat16), v_ref[0]).astype(jnp.bfloat16)
    high = total.astype(jnp.bfloat16).astype(jnp.float32)
    low = total - high
    lane = lax.broadcasted_iota(jnp.int32, (nodes, LANES), 1)
    for block in range(blocks):
        stats = jnp.zeros((nodes, LANES), jnp.float32)
        for head in range(heads_here):
            at = (block * heads_here + head) * nodes
            out_ref[block, head, 0] = summed[at : at + nodes]
            stats = jnp.where(lane == head, top[at : at + nodes], stats)
            stats = jnp.where(lane == heads_here + head, high[at : at + nodes], stats)
            stats = jnp.where(lane == 2 * heads_here + head, low[at : at + nodes], stats)
        out_ref[block, heads_here, 0] = stats.astype(jnp.bfloat16)


def attend(left, every_query, keys, values):
    column_count, requests, nodes, width_here = every_query.shape
    heads_here = width_here // HEAD_WIDTH
    kv_heads = keys.shape[2] // HEAD_WIDTH
    blocks = column_count // kv_heads
    prefix_here = keys.shape[1]
    return pl.pallas_call(
        functools.partial(attend_kernel, blocks * heads_here),
        grid_spec=pltpu.PrefetchScalarGridSpec(
            num_scalar_prefetch=1,
            grid=(requests, kv_heads),
            in_specs=[
                pl.BlockSpec((blocks, 1, nodes, width_here), lambda r, g, m: (g, r, 0, 0)),
                pl.BlockSpec((1, prefix_here, HEAD_WIDTH), lambda r, g, m: (r, 0, g)),
                pl.BlockSpec((1, prefix_here, HEAD_WIDTH), lambda r, g, m: (r, 0, g)),
            ],
            out_specs=pl.BlockSpec(
                (blocks, heads_here + 1, 1, nodes, HEAD_WIDTH), lambda r, g, m: (g, 0, r, 0, 0)
            ),
        ),
        out_shape=jax.ShapeDtypeStruct(
            (column_count, heads_here + 1, requests, nodes, HEAD_WIDTH), jnp.bfloat16
        ),
        compiler_params=params(),
        cost_estimate=pl.CostEstimate(
            flops=4 * requests * nodes * width_here * column_count * prefix_here,
            bytes_accessed=4 * requests * prefix_here * kv_heads * HEAD_WIDTH,
            transcendentals=requests * nodes * heads_here * column_count * prefix_here,
        ),
        name="attend",
    )(left, every_query, keys, values)


def merge_kernel(kv_ref, got_ref, q_ref, tk_ref, tv_ref, linked_ref, out_ref):
    sources, more, _, nodes, _ = got_ref.shape
    heads = more - 1
    query = jnp.concatenate(
        [q_ref[0, :, h * HEAD_WIDTH : (h + 1) * HEAD_WIDTH] for h in range(heads)], axis=0
    )
    linked = jnp.concatenate([linked_ref[0]] * heads, axis=0) > 0.5
    scores = dot(query, tk_ref[0], CONTRACT_LAST) * INV_ROOT
    top = jnp.max(jnp.where(linked, scores, NEG_FILL), axis=1, keepdims=True)
    tops, totals = [], []
    for source in range(sources):
        stats = got_ref[source, heads, 0].astype(jnp.float32)

        def columns(first):
            return jnp.concatenate([stats[:, first + h : first + h + 1] for h in range(heads)], axis=0)

        tops.append(columns(0))
        totals.append(columns(heads) + columns(2 * heads))
    for value in tops:
        top = jnp.maximum(top, value)
    weights = jnp.where(linked, jnp.exp(scores - top), 0.0)
    total = jnp.sum(weights, axis=1, keepdims=True)
    summed = dot(weights.astype(jnp.bfloat16), tv_ref[0])
    for source in range(sources):
        factor = jnp.exp(tops[source] - top)
        total = total + totals[source] * factor
        part = jnp.concatenate([got_ref[source, h, 0] for h in range(heads)], axis=0)
        summed = summed + part.astype(jnp.float32) * factor
    attended = (summed / total).astype(jnp.bfloat16)
    for h in range(heads):
        out_ref[0, :, h * HEAD_WIDTH : (h + 1) * HEAD_WIDTH] = attended[h * nodes : (h + 1) * nodes]


def merge(kv_group, got, queries, tree_keys, tree_values, linked):
    sources, more, requests, nodes, _ = got.shape
    width_here = queries.shape[2]
    return pl.pallas_call(
        merge_kernel,
        grid_spec=pltpu.PrefetchScalarGridSpec(
            num_scalar_prefetch=1,
            grid=(requests,),
            in_specs=[
                pl.BlockSpec((sources, more, 1, nodes, HEAD_WIDTH), lambda r, k: (0, 0, r, 0, 0)),
                pl.BlockSpec((1, nodes, width_here), lambda r, k: (r, 0, 0)),
                pl.BlockSpec((1, nodes, HEAD_WIDTH), lambda r, k: (r, 0, k[0])),
                pl.BlockSpec((1, nodes, HEAD_WIDTH), lambda r, k: (r, 0, k[0])),
                pl.BlockSpec((1, nodes, nodes), lambda r, k: (r, 0, 0)),
            ],
            out_specs=pl.BlockSpec((1, nodes, width_here), lambda r, k: (r, 0, 0)),
        ),
        out_shape=jax.ShapeDtypeStruct((requests, nodes, width_here), jnp.bfloat16),
        compiler_params=params(),
        name="merge",
    )(kv_group, got, queries, tree_keys, tree_values, linked)


def project_kernel(slot_ref, x_ref, down_ref, w_ref, out_ref, shrunk_ref):
    requests, nodes, width_here = x_ref.shape
    wide = w_ref.shape[1]

    @pl.when(pl.program_id(0) == 0)
    def _():
        shrunk_ref[...] = jnp.zeros_like(shrunk_ref)
        for r in range(requests):
            part = dot(x_ref[r], down_ref[slot_ref[r]], CONTRACT_LAST)
            shrunk_ref[r * nodes : (r + 1) * nodes, :ADAPTER_RANK] = part.astype(jnp.bfloat16)

    rows = x_ref[...].reshape(requests * nodes, width_here)
    out_ref[0, :, :wide] = dot(rows, w_ref[...]).astype(jnp.bfloat16)
    out_ref[0, :, wide:] = shrunk_ref[...]


def project(slot_code, attended, down, weight, columns):
    requests, nodes, width_here = attended.shape
    slots = down.shape[0]
    wide = weight.shape[1] // columns
    rows = requests * nodes
    return pl.pallas_call(
        project_kernel,
        grid_spec=pltpu.PrefetchScalarGridSpec(
            num_scalar_prefetch=1,
            grid=(columns,),
            in_specs=[
                pl.BlockSpec((requests, nodes, width_here), lambda c, s: (0, 0, 0)),
                pl.BlockSpec((slots, ADAPTER_RANK, width_here), lambda c, s: (0, 0, 0)),
                pl.BlockSpec((width_here, wide), lambda c, s: (0, c)),
            ],
            out_specs=pl.BlockSpec((1, rows, wide + LANES), lambda c, s: (c, 0, 0)),
            scratch_shapes=[pltpu.VMEM((rows, LANES), jnp.bfloat16)],
        ),
        out_shape=jax.ShapeDtypeStruct((columns, rows, wide + LANES), jnp.bfloat16),
        compiler_params=params(),
        name="project",
    )(slot_code, attended, down, weight)


def raise_kernel(slot_ref, base_ref, up_ref, out_ref):
    wide = out_ref.shape[2]
    shrunk = base_ref[:, wide : wide + ADAPTER_RANK]
    raised = dot(shrunk, up_ref[0])
    out_ref[0] = (base_ref[:, :wide].astype(jnp.float32) + ADAPTER_SCALE * raised).astype(
        jnp.bfloat16
    )


def finish(slot_code, base, up, requests):
    rows, wider = base.shape
    wide = wider - LANES
    nodes = rows // requests
    return pl.pallas_call(
        raise_kernel,
        grid_spec=pltpu.PrefetchScalarGridSpec(
            num_scalar_prefetch=1,
            grid=(requests,),
            in_specs=[
                pl.BlockSpec((nodes, wider), lambda r, s: (r, 0)),
                pl.BlockSpec((1, ADAPTER_RANK, wide), lambda r, s: (s[r], 0, 0)),
            ],
            out_specs=pl.BlockSpec((1, nodes, wide), lambda r, s: (r, 0, 0)),
        ),
        out_shape=jax.ShapeDtypeStruct((requests, nodes, wide), jnp.bfloat16),
        compiler_params=params(),
        name="finish",
    )(slot_code, base, up)


def per_device(
    queries,
    prefix_key_cache,
    prefix_value_cache,
    tree_node_keys,
    tree_node_values,
    lengths,
    parents,
    request_adapter_index,
    output_projection_weight,
    adapter_down_weight,
    adapter_up_weight,
):
    requests, nodes, width_here = queries.shape
    columns = lax.axis_size("mp")
    column = lax.axis_index("mp")
    heads_here = width_here // HEAD_WIDTH
    prefix_here = prefix_key_cache.shape[1]
    kv_heads = prefix_key_cache.shape[2] // HEAD_WIDTH
    group_size = heads_here * columns // kv_heads
    batch_size = lax.axis_size("batch")
    batch_row = lax.axis_index("batch")
    present, rank, _ = adapter_down_weight.shape

    every_ids = request_adapter_index.reshape(batch_size, requests)
    is_mine = every_ids // present == batch_row
    counted = is_mine.astype(jnp.int32)
    slot_rank = jnp.cumsum(counted, axis=1) - counted
    slot_ids = jnp.arange(CAP, dtype=jnp.int32)
    select = (slot_rank[:, None, :] == slot_ids[None, :, None]) & is_mine[:, None, :]
    picked = jnp.sum(jnp.where(select, (every_ids % present)[:, None, :], 0), axis=2).reshape(-1)
    send_down, send_up = pick(picked, adapter_down_weight, adapter_up_weight)
    down = lax.all_to_all(send_down, "batch", split_axis=0, concat_axis=0, tiled=True)
    up = lax.all_to_all(send_up, "batch", split_axis=0, concat_axis=0, tiled=True)
    mine_ids = lax.dynamic_slice_in_dim(request_adapter_index, batch_row * requests, requests)
    my_owner = mine_ids // present
    positions = jnp.arange(requests, dtype=jnp.int32)
    earlier = (my_owner[:, None] == my_owner[None, :]) & (positions[None, :] < positions[:, None])
    slot_code = my_owner * CAP + jnp.sum(earlier.astype(jnp.int32), axis=1)

    every_query = lax.all_gather(queries, "mp", axis=0)
    left = lengths - column * prefix_here
    partial = attend(left, every_query, prefix_key_cache, prefix_value_cache)
    got = lax.all_to_all(partial, "mp", split_axis=0, concat_axis=0, tiled=True)
    kv_group = (column * heads_here // group_size).reshape(1)
    attended = merge(
        kv_group, got, queries, tree_node_keys, tree_node_values, ancestors(parents)
    )
    shares = project(slot_code, attended, down, output_projection_weight, columns)
    base = lax.psum_scatter(shares, "mp", scatter_dimension=0, tiled=False)
    return finish(slot_code, base, up, requests)


def solution(mesh):
    return jax.shard_map(
        per_device,
        mesh=mesh,
        in_specs=(
            P(("groups", "batch"), None, "mp"),
            P(("groups", "batch"), "mp", None),
            P(("groups", "batch"), "mp", None),
            P(("groups", "batch"), None, None),
            P(("groups", "batch"), None, None),
            P(("groups", "batch")),
            P(("groups", "batch"), None),
            P("groups"),
            P("mp", None),
            P("batch", None, "mp"),
            P("batch", None, "mp"),
        ),
        out_specs=P(("groups", "batch"), None, "mp"),
        check_vma=False,
    )
```

time: 186 us -> 167 us (0.90)
  matrix products: 43.5 us -> 0.76 us
  blocking collectives: 11.5 us -> 51.3 us
  Pallas kernels: 0 us -> 35.2 us
  local copies, waits for them, and re-layouts: 32.1 us -> 3.89 us
  starting transfers between devices: 19.7 us -> 8.27 us
  waiting for transfers between devices: 58.6 us -> 52.2 us
  other arithmetic: 5.87 us -> 1.36 us
    all_to_all x0 -> x1, blocking collectives: none -> 51.3 us  [per_device(): lax.all_to_all(send_up, 'batch', split_axis=0, concat_axis=0, tiled=True)]
    dot_general x17 -> x3, matrix products: 43.5 us -> 0.76 us  [ancestors(): jnp.einsum('rnm,rmk->rnk', step, step, preferred_element_type=jnp.float32)]
    all_to_all x4 -> x1, waiting for transfers between devices: 48.9 us -> 10.5 us  [per_device(): got = lax.all_to_all(partial, 'mp', split_axis=0, concat_axis=0, tiled=True)]
    pallas_call x0 -> x5, Pallas kernels: none -> 35.2 us  [the longest x1 16.4 us: attend(): pl.pallas_call(functools.partial(attend_kernel, blocks * heads_here), gri...]
    all_gather x1, waiting for transfers between devices: 0.27 us -> 20.5 us  [per_device(): every_query = lax.all_gather(queries, 'mp', axis=0)]
    reshape x8 -> x2, local copies, waits for them, and re-layouts: 18.8 us -> 0.17 us  [the longest x1 0.09 us: per_device(): jnp.sum(jnp.where(select, (every_ids % present)[:, None, :], 0), axis=2)]
    all_to_all x1, waiting for transfers between devices: 8.63 us -> 20.5 us  [per_device(): lax.all_to_all(send_down, 'batch', split_axis=0, concat_axis=0, tiled=True)]
    psum x1 -> x0, blocking collectives: 11.5 us -> none  [per_device(): shrunk = lax.psum(shrink_part.astype(jnp.bfloat16), 'mp')]
  transfers between devices with their start and end apart: 7 -> 4, of which waited for: 5 -> 3; matrix products, arithmetic and copies ran while one was open for 34% -> 1% of each run, Pallas kernels for 0% -> 4%
where the time goes in v1:
time: 167 us; the launch traced here: 166 us
  waiting for transfers between devices  52.2 us (31%)
  blocking collectives  51.3 us (31%)
  Pallas kernels  35.2 us (21%)
  between operations  13.5 us (8%)
  starting transfers between devices  8.27 us (5%)
  local copies, waits for them, and re-layouts  3.89 us (2%)
    all_to_all x1, blocking collectives, per_device(): lax.all_to_all(send_up, 'batch', split_axis=0, concat_axis=0, tiled=True)  51.3 us
    all_to_all x1, waiting for transfers between devices, per_device(): lax.all_to_all(send_down, 'batch', split_axis=0, concat_axis=0, tiled=True)  20.5 us
    all_gather x1, waiting for transfers between devices, per_device(): every_query = lax.all_gather(queries, 'mp', axis=0)  20.5 us
    pallas_call x1, Pallas kernels, attend(): pl.pallas_call(functools.partial(attend_kernel, blocks * heads_here), gri...  16.4 us
    all_to_all x1, waiting for transfers between devices, per_device(): got = lax.all_to_all(partial, 'mp', split_axis=0, concat_axis=0, tiled=True)  10.5 us
    pallas_call x1, Pallas kernels, project(): pl.pallas_call(project_kernel, grid_spec=pltpu.PrefetchScalarGridSpec(num...  9.24 us
    all_to_all x1, starting transfers between devices, per_device(): lax.all_to_all(send_down, 'batch', split_axis=0, concat_axis=0, tiled=True)  4.6 us
    pallas_call x1, Pallas kernels, merge(): pl.pallas_call(merge_kernel, grid_spec=pltpu.PrefetchScalarGridSpec(num_s...  3.81 us
  transfers between devices with their start and end apart: 4, of which 3 were waited for; matrix products, arithmetic and copies ran while one was open for 1% of the time, Pallas kernels for 4%

profile of v1, /device:TPU:0, one launch (start us, length us, event | category | flops | bytes accessed | tf_op | source)
XLA Modules:
  0.0 166.5 jit_solution(12724100674688504538)
XLA Ops:
  6.5 0.0 all-gather.3.cloned.1.call-start
  6.5 0.7 all-gather.3.cloned.1.call-update
  7.3 0.7 broadcast_subtract_fusion.meta_ref
  7.9 20.5 %all-gather.3.cloned.1.call-done = bf16[16,32,1024]{2,1,0:T(8,128)(2,1)} async-done(((bf16[4,32,1024]{2,1,0:T(8,128)(2,1)}), bf16[16,32,1024]{2,1,0:T(8,128)(2,1)}) %all-gather.3.cloned.1.call-update) | async-done | bytes 1048592 | tf_op jit(solution)/shard_map/all_gather | solution.py:310
  28.4 0.0 copy-start.3
  28.4 1.2 copy-done.3
  29.6 16.4 %attend.1 = bf16[4,9,4,32,128]{4,3,2,1,0:T(8,128)(2,1)} custom-call(s32[4]{0:T(128)S(1)} %broadcast_subtract_fusion.meta_ref, bf16[4,4,32,1024]{3,2,1,0:T(8,128)(2,1)S(1)} %bitcast.7, bf16[4,1024,512]{2,1,0:T(8,128)(2,1)} %k_ref.1, bf16[4,1024,512]{2,1,0:T(8,128)(2,1)} %v_ref.1), custom_call_target="tpu_custom_call" | custom-call | flops 2147483648 | bytes 8388608 | tf_op jit(solution)/shard_map/attend/pallas_call | solution.py:117
  46.0 0.0 copy-start.8
  46.0 0.0 copy-start.2
  46.0 0.0 copy-start.5
  46.0 3.7 %all-to-all-start = ((bf16[4,9,4,32,128]{4,3,2,1,0:T(8,128)(2,1)}), bf16[4,9,4,32,128]{4,3,2,1,0:T(8,128)(2,1)S(1)}, u32[]{:S(2)}, u32[]{:S(2)}) async-start(bf16[4,9,4,32,128]{4,3,2,1,0:T(8,128)(2,1)} %attend.1), calls=%async_computation | async-start | bytes 2359296 | tf_op jit(solution)/shard_map/all_to_all | solution.py:313
  49.7 0.0 copy-start.9
  49.7 0.0 copy-start.1
  49.7 0.0 copy-start.6
  49.7 0.0 copy-start.7
  49.7 0.0 copy-done.8
  49.7 0.1 reshape.117
  49.8 0.2 reduce_window_sum.11
  50.0 0.1 select_reduce_fusion
  50.2 0.1 copy.12
  50.3 0.1 reshape.118.picked_ref
  50.4 0.0 copy-done.2
  50.4 0.0 copy-done.5
  50.4 3.4 %pick.1 = (bf16[8,64,1024]{2,1,0:T(8,128)(2,1)}, bf16[8,64,2048]{2,1,0:T(8,128)(2,1)S(1)}) custom-call(s32[8]{0:T(128)S(1)} %reshape.118.picked_ref, bf16[4,64,1024]{2,1,0:T(8,128)(2,1)S(1)} %copy-done.5, bf16[4,64,2048]{2,1,0:T(8,128)(2,1)S(1)} %copy-done.2), custom_call_target="tpu_custom_call" | custom-call | tf_op jit(solution)/shard_map/pick/pallas_call | solution.py:55
  53.7 0.0 copy-start
  53.7 1.3 copy-done
  55.0 10.5 %all-to-all-done.got_ref = bf16[4,9,4,32,128]{4,3,2,1,0:T(8,128)(2,1)S(1)} async-done(((bf16[4,9,4,32,128]{4,3,2,1,0:T(8,128)(2,1)}), bf16[4,9,4,32,128]{4,3,2,1,0:T(8,128)(2,1)S(1)}, u32[]{:S(2)}, u32[]{:S(2)}) %all-to-all-start) | async-done | bytes 1179680 | tf_op jit(solution)/shard_map/all_to_all | solution.py:313
  65.5 4.6 %all-to-all-start.1 = ((bf16[8,64,1024]{2,1,0:T(8,128)(2,1)}), bf16[8,64,1024]{2,1,0:T(8,128)(2,1)S(1)}, u32[]{:S(2)}, u32[]{:S(2)}) async-start(bf16[8,64,1024]{2,1,0:T(8,128)(2,1)} %get-tuple-element.7), calls=%async_computation.1 | async-start | bytes 2097152 | tf_op jit(solution)/shard_map/all_to_all | solution.py:302
  70.1 0.0 reduce-scatter.2.cloned.1.call-start
  70.1 0.1 and_select_fusion
  70.2 0.2 convert_reduce_fusion
  70.4 0.1 multiply_add_fusion.slot_ref
  70.5 0.0 copy-done.9
  70.5 0.4 fusion.1
  70.8 0.3 fusion.3
  71.1 0.1 convolution_minimum_fusion.linked_ref
  71.2 0.0 copy-done.1
  71.2 0.0 copy-done.6
  71.3 0.0 copy-done.7
  71.3 3.8 %merge.1.x_ref = bf16[4,32,1024]{2,1,0:T(8,128)(2,1)S(1)} custom-call(s32[1]{0:T(128)} %bitcast.kv_ref, bf16[4,9,4,32,128]{4,3,2,1,0:T(8,128)(2,1)S(1)} %all-to-all-done.got_ref, bf16[4,32,1024]{2,1,0:T(8,128)(2,1)S(1)} %copy-done.1, bf16[4,32,512]{2,1,0:T(8,128)(2,1)S(1)} %copy-done.6, bf16[4,32,512]{2,1,0:T(8,128)(2,1)S(1)} %copy-done.7, ...), custom_call_target="tpu_custom_call" | custom-call | tf_op jit(solution)/shard_map/merge/pallas_call | solution.py:180
  75.1 20.5 %all-to-all-done.1.down_ref = bf16[8,64,1024]{2,1,0:T(8,128)(2,1)S(1)} async-done(((bf16[8,64,1024]{2,1,0:T(8,128)(2,1)}), bf16[8,64,1024]{2,1,0:T(8,128)(2,1)S(1)}, u32[]{:S(2)}, u32[]{:S(2)}) %all-to-all-start.1) | async-done | bytes 1048608 | tf_op jit(solution)/shard_map/all_to_all | solution.py:302
  95.6 9.2 %project.1 = bf16[4,128,2176]{2,1,0:T(8,128)(2,1)} custom-call(s32[4]{0:T(128)S(1)} %multiply_add_fusion.slot_ref, bf16[4,32,1024]{2,1,0:T(8,128)(2,1)S(1)} %merge.1.x_ref, bf16[8,64,1024]{2,1,0:T(8,128)(2,1)S(1)} %all-to-all-done.1.down_ref, bf16[1024,8192]{1,0:T(8,128)(2,1)} %w_ref.1), custom_call_target="tpu_custom_call" | custom-call | tf_op jit(solution)/shard_map/project/pallas_call | solution.py:221
  104.9 0.0 reduce-scatter.2.cloned.1.call-update
  104.9 51.3 %all_to_all.15.up_ref = bf16[8,64,2048]{2,1,0:T(8,128)(2,1)S(1)} all-to-all(bf16[8,64,2048]{2,1,0:T(8,128)(2,1)} %copy-done), channel_id=1, replica_groups=mesh['groups'=2,'batch'=4,'mp'=4] {'batch'}, dimensions={0} | all-to-all | bytes 4194304 | tf_op jit(solution)/shard_map/all_to_all | solution.py:303
  156.2 0.0 reduce-scatter.2.cloned.1.call-done
  156.2 0.0 copy-start.4
  156.2 1.1 copy-done.4
  157.2 2.4 %finish.1 = bf16[4,32,2048]{2,1,0:T(8,128)(2,1)} custom-call(s32[4]{0:T(128)S(1)} %multiply_add_fusion.slot_ref, bf16[128,2176]{1,0:T(8,128)(2,1)S(1)} %bitcast.8, bf16[8,64,2048]{2,1,0:T(8,128)(2,1)S(1)} %all_to_all.15.up_ref), custom_call_target="tpu_custom_call" | custom-call | tf_op jit(solution)/shard_map/finish/pallas_call | solution.py:253
  (3 shorter events, 0.0 us)
Async XLA Ops:
  6.5 21.8 %all-gather.3.cloned.1.call-start = ((), (), s32[]{:S(2)}) async-start(), calls=%async_computation.5 | async-start | bytes 1310720 | tf_op jit(solution)/shard_map/all_gather | solution.py:310
  28.4 1.2 copy-start.3
  46.0 3.7 %copy-start.8 = (s32[16]{0:T(128)S(1)}, s32[16]{0:T(128)}, u32[]{:S(2)}) copy-start(s32[16]{0:T(128)} %param.18) | copy-start | bytes 196
  46.0 4.4 %copy-start.2 = (bf16[4,64,2048]{2,1,0:T(8,128)(2,1)S(1)}, bf16[4,64,2048]{2,1,0:T(8,128)(2,1)}, u32[]{:S(2)}) copy-start(bf16[4,64,2048]{2,1,0:T(8,128)(2,1)} %up_ref.1) | copy-start | bytes 3145732
  46.0 4.4 %copy-start.5 = (bf16[4,64,1024]{2,1,0:T(8,128)(2,1)S(1)}, bf16[4,64,1024]{2,1,0:T(8,128)(2,1)}, u32[]{:S(2)}) copy-start(bf16[4,64,1024]{2,1,0:T(8,128)(2,1)} %down_ref.1) | copy-start | bytes 1572868
  46.0 19.5 %all-to-all-start = ((bf16[4,9,4,32,128]{4,3,2,1,0:T(8,128)(2,1)}), bf16[4,9,4,32,128]{4,3,2,1,0:T(8,128)(2,1)S(1)}, u32[]{:S(2)}, u32[]{:S(2)}) async-start(bf16[4,9,4,32,128]{4,3,2,1,0:T(8,128)(2,1)} %attend.1), calls=%async_computation | async-start | bytes 2359296 | tf_op jit(solution)/shard_map/all_to_all | solution.py:313
  49.7 20.8 %copy-start.9 = (s32[4,32]{1,0:T(4,128)S(1)}, s32[4,32]{1,0:T(4,128)}, u32[]{:S(2)}) copy-start(s32[4,32]{1,0:T(4,128)} %param.17) | copy-start | bytes 1540
  49.7 21.6 %copy-start.1 = (bf16[4,32,1024]{2,1,0:T(8,128)(2,1)S(1)}, bf16[4,32,1024]{2,1,0:T(8,128)(2,1)}, u32[]{:S(2)}) copy-start(bf16[4,32,1024]{2,1,0:T(8,128)(2,1)} %q_ref.1) | copy-start | bytes 786436
  49.7 21.6 %copy-start.6 = (bf16[4,32,512]{2,1,0:T(8,128)(2,1)S(1)}, bf16[4,32,512]{2,1,0:T(8,128)(2,1)}, u32[]{:S(2)}) copy-start(bf16[4,32,512]{2,1,0:T(8,128)(2,1)} %tk_ref.1) | copy-start | bytes 393220
  49.7 21.5 %copy-start.7 = (bf16[4,32,512]{2,1,0:T(8,128)(2,1)S(1)}, bf16[4,32,512]{2,1,0:T(8,128)(2,1)}, u32[]{:S(2)}) copy-start(bf16[4,32,512]{2,1,0:T(8,128)(2,1)} %tv_ref.1) | copy-start | bytes 393220
  53.7 1.3 copy-start
  65.5 30.1 %all-to-all-start.1 = ((bf16[8,64,1024]{2,1,0:T(8,128)(2,1)}), bf16[8,64,1024]{2,1,0:T(8,128)(2,1)S(1)}, u32[]{:S(2)}, u32[]{:S(2)}) async-start(bf16[8,64,1024]{2,1,0:T(8,128)(2,1)} %get-tuple-element.7), calls=%async_computation.1 | async-start | bytes 2097152 | tf_op jit(solution)/shard_map/all_to_all | solution.py:302
  70.1 86.1 %reduce-scatter.2.cloned.1.call-start = ((), (), s32[]{:S(2)}) async-start(), calls=%async_computation.4 | async-start | bytes 2785280 | tf_op jit(solution)/shard_map/reduce_scatter | solution.py:319
  156.2 1.1 copy-start.4
Sparse Core Ops, SparseCore 0:
  8.9 19.4 all-gather.2
  105.0 30.4 reduce-scatter.1

commit v2 on v1

--- a/solution.py
+++ b/solution.py
@@ -43,40 +43,64 @@
     return reached
 
 
-def pick_kernel(picked_ref, down_ref, up_ref, down_out, up_out):
-    down_out[...] = down_ref[...]
-    up_out[...] = up_ref[...]
-
-
-def pick(picked, down, up):
-    slots = picked.shape[0]
-    present, rank, width = down.shape
-    up_width = up.shape[2]
-    return pl.pallas_call(
-        pick_kernel,
-        grid_spec=pltpu.PrefetchScalarGridSpec(
-            num_scalar_prefetch=1,
-            grid=(slots,),
-            in_specs=[
-                pl.BlockSpec((1, rank, width), lambda s, p: (p[s], 0, 0)),
-                pl.BlockSpec((1, rank, up_width), lambda s, p: (p[s], 0, 0)),
-            ],
-            out_specs=[
-                pl.BlockSpec((1, rank, width), lambda s, p: (s, 0, 0)),
-                pl.BlockSpec((1, rank, up_width), lambda s, p: (s, 0, 0)),
-            ],
-        ),
-        out_shape=[
-            jax.ShapeDtypeStruct((slots, rank, width), down.dtype),
-            jax.ShapeDtypeStruct((slots, rank, up_width), up.dtype),
-        ],
+def pick_kernel(shifts, picked_ref, left_ref, down_ref, up_ref, left_out, *rest):
+    firsts, seconds, sems = rest[:shifts], rest[shifts : 2 * shifts], rest[2 * shifts]
+    half = up_ref.shape[2] // 2
+    width = down_ref.shape[2]
+    copies = []
+    for shift in range(shifts):
+        for slot in range(CAP):
+            at = shift * CAP + slot
+            index = picked_ref[at]
+            pairs = (
+                (up_ref.at[index, :, pl.ds(0, half)], firsts[shift].at[slot, :, pl.ds(0, half)]),
+                (down_ref.at[index], firsts[shift].at[slot, :, pl.ds(half, width)]),
+                (up_ref.at[index, :, pl.ds(half, half)], seconds[shift].at[slot]),
+            )
+            for which, (source, target) in enumerate(pairs):
+                copies.append(pltpu.make_async_copy(source, target, sems.at[which, at]))
+    for copy in copies:
+        copy.start()
+    for r in range(left_ref.shape[0]):
+        left_out[r] = left_ref[r]
+    for copy in copies:
+        copy.wait()
+
+
+def pick(picked, left, down, up):
+    shifts = picked.shape[0] // CAP
+    hbm = pl.BlockSpec(memory_space=pl.ANY)
+    smem = pl.BlockSpec(memory_space=pltpu.SMEM)
+    half = up.shape[2] // 2
+    first = jax.ShapeDtypeStruct((CAP, up.shape[1], half + down.shape[2]), up.dtype)
+    second = jax.ShapeDtypeStruct((CAP, up.shape[1], half), up.dtype)
+    out = pl.pallas_call(
+        functools.partial(pick_kernel, shifts),
+        in_specs=[smem, smem, hbm, hbm],
+        out_specs=[smem] + [hbm] * (2 * shifts),
+        out_shape=[jax.ShapeDtypeStruct(left.shape, left.dtype)]
+        + [first] * shifts
+        + [second] * shifts,
+        scratch_shapes=[pltpu.SemaphoreType.DMA((3, shifts * CAP))],
         compiler_params=params(),
         name="pick",
-    )(picked, down, up)
-
-
-def attend_kernel(group_size, meta_ref, q_ref, k_ref, v_ref, out_ref):
-    blocks, _, nodes, width_here = q_ref.shape
+    )(picked, left, down, up)
+    return out[0], out[1 : 1 + shifts], out[1 + shifts :]
+
+
+def exchange(blocks, axis):
+    size = len(blocks)
+    got = [blocks[0]]
+    for shift in range(1, size):
+        pairs = [(i, (i + shift) % size) for i in range(size)]
+        got.append(lax.ppermute(blocks[shift], axis, pairs))
+    return got
+
+
+def attend_kernel(blocks, meta_ref, *refs):
+    q_refs = refs[:blocks]
+    k_ref, v_ref, out_ref = refs[blocks:]
+    _, _, nodes, width_here = q_refs[0].shape
     heads_here = width_here // HEAD_WIDTH
     request = pl.program_id(0)
     positions = k_ref.shape[1]
@@ -84,7 +108,7 @@
     rows = []
     for block in range(blocks):
         for head in range(heads_here):
-            rows.append(q_ref[block, 0, :, head * HEAD_WIDTH : (head + 1) * HEAD_WIDTH])
+            rows.append(q_refs[block][0, 0, :, head * HEAD_WIDTH : (head + 1) * HEAD_WIDTH])
     query = jnp.concatenate(rows, axis=0)
     scores = dot(query, k_ref[0], CONTRACT_LAST) * INV_ROOT
     place = lax.broadcasted_iota(jnp.int32, (1, positions), 1)
@@ -108,19 +132,26 @@
         out_ref[block, heads_here, 0] = stats.astype(jnp.bfloat16)
 
 
-def attend(left, every_query, keys, values):
+def attend(meta, every_query, keys, values):
     column_count, requests, nodes, width_here = every_query.shape
     heads_here = width_here // HEAD_WIDTH
     kv_heads = keys.shape[2] // HEAD_WIDTH
     blocks = column_count // kv_heads
     prefix_here = keys.shape[1]
+
+    def query_spec(block):
+        def index(r, g, m):
+            return (m[requests] - (g * blocks + block) + column_count) % column_count, r, 0, 0
+
+        return pl.BlockSpec((1, 1, nodes, width_here), index)
+
     return pl.pallas_call(
-        functools.partial(attend_kernel, blocks * heads_here),
+        functools.partial(attend_kernel, blocks),
         grid_spec=pltpu.PrefetchScalarGridSpec(
             num_scalar_prefetch=1,
             grid=(requests, kv_heads),
             in_specs=[
-                pl.BlockSpec((blocks, 1, nodes, width_here), lambda r, g, m: (g, r, 0, 0)),
+                *[query_spec(block) for block in range(blocks)],
                 pl.BlockSpec((1, prefix_here, HEAD_WIDTH), lambda r, g, m: (r, 0, g)),
                 pl.BlockSpec((1, prefix_here, HEAD_WIDTH), lambda r, g, m: (r, 0, g)),
             ],
@@ -138,7 +169,7 @@
             transcendentals=requests * nodes * heads_here * column_count * prefix_here,
         ),
         name="attend",
-    )(left, every_query, keys, values)
+    )(meta, *[every_query] * blocks, keys, values)
 
 
 def merge_kernel(kv_ref, got_ref, q_ref, tk_ref, tv_ref, linked_ref, out_ref):
@@ -213,9 +244,10 @@
     out_ref[0, :, wide:] = shrunk_ref[...]
 
 
-def project(slot_code, attended, down, weight, columns):
+def project(slot_code, attended, maps, weight, columns):
     requests, nodes, width_here = attended.shape
-    slots = down.shape[0]
+    slots = maps.shape[0]
+    down_block = maps.shape[2] // width_here - 1
     wide = weight.shape[1] // columns
     rows = requests * nodes
     return pl.pallas_call(
@@ -225,7 +257,7 @@
             grid=(columns,),
             in_specs=[
                 pl.BlockSpec((requests, nodes, width_here), lambda c, s: (0, 0, 0)),
-                pl.BlockSpec((slots, ADAPTER_RANK, width_here), lambda c, s: (0, 0, 0)),
+                pl.BlockSpec((slots, ADAPTER_RANK, width_here), lambda c, s: (0, 0, down_block)),
                 pl.BlockSpec((width_here, wide), lambda c, s: (0, c)),
             ],
             out_specs=pl.BlockSpec((1, rows, wide + LANES), lambda c, s: (c, 0, 0)),
@@ -234,37 +266,36 @@
         out_shape=jax.ShapeDtypeStruct((columns, rows, wide + LANES), jnp.bfloat16),
         compiler_params=params(),
         name="project",
-    )(slot_code, attended, down, weight)
-
-
-def raise_kernel(slot_ref, base_ref, up_ref, out_ref):
+    )(slot_code, attended, maps, weight)
+
+
+def raise_kernel(slot_ref, base_ref, first_ref, second_ref, out_ref):
     wide = out_ref.shape[2]
+    half = wide // 2
     shrunk = base_ref[:, wide : wide + ADAPTER_RANK]
-    raised = dot(shrunk, up_ref[0])
-    out_ref[0] = (base_ref[:, :wide].astype(jnp.float32) + ADAPTER_SCALE * raised).astype(
-        jnp.bfloat16
-    )
-
-
-def finish(slot_code, base, up, requests):
+    for at, up_ref in ((0, first_ref), (half, second_ref)):
+        raised = dot(shrunk, up_ref[0])
+        projected = base_ref[:, at : at + half].astype(jnp.float32)
+        out_ref[0, :, at : at + half] = (projected + ADAPTER_SCALE * raised).astype(jnp.bfloat16)
+
+
+def finish(slot_code, base, maps, rest, requests):
     rows, wider = base.shape
     wide = wider - LANES
     nodes = rows // requests
+    up_spec = pl.BlockSpec((1, ADAPTER_RANK, wide // 2), lambda r, s: (s[r], 0, 0))
     return pl.pallas_call(
         raise_kernel,
         grid_spec=pltpu.PrefetchScalarGridSpec(
             num_scalar_prefetch=1,
             grid=(requests,),
-            in_specs=[
-                pl.BlockSpec((nodes, wider), lambda r, s: (r, 0)),
-                pl.BlockSpec((1, ADAPTER_RANK, wide), lambda r, s: (s[r], 0, 0)),
-            ],
+            in_specs=[pl.BlockSpec((nodes, wider), lambda r, s: (r, 0)), up_spec, up_spec],
             out_specs=pl.BlockSpec((1, nodes, wide), lambda r, s: (r, 0, 0)),
         ),
         out_shape=jax.ShapeDtypeStruct((requests, nodes, wide), jnp.bfloat16),
         compiler_params=params(),
         name="finish",
-    )(slot_code, base, up)
+    )(slot_code, base, maps, rest)
 
 
 def per_device(
@@ -297,27 +328,33 @@
     slot_rank = jnp.cumsum(counted, axis=1) - counted
     slot_ids = jnp.arange(CAP, dtype=jnp.int32)
     select = (slot_rank[:, None, :] == slot_ids[None, :, None]) & is_mine[:, None, :]
-    picked = jnp.sum(jnp.where(select, (every_ids % present)[:, None, :], 0), axis=2).reshape(-1)
-    send_down, send_up = pick(picked, adapter_down_weight, adapter_up_weight)
-    down = lax.all_to_all(send_down, "batch", split_axis=0, concat_axis=0, tiled=True)
-    up = lax.all_to_all(send_up, "batch", split_axis=0, concat_axis=0, tiled=True)
+    picked = jnp.sum(jnp.where(select, (every_ids % present)[:, None, :], 0), axis=2)
+    target = (batch_row + jnp.arange(batch_size, dtype=jnp.int32)) % batch_size
+    chosen = target[:, None] == jnp.arange(batch_size, dtype=jnp.int32)[None, :]
+    picked = jnp.sum(jnp.where(chosen[:, :, None], picked[None], 0), axis=1).reshape(-1)
+    left, firsts, seconds = pick(
+        picked, lengths - column * prefix_here, adapter_down_weight, adapter_up_weight
+    )
+    maps = jnp.concatenate(exchange(firsts, "batch"), axis=0)
+    rest = jnp.concatenate(exchange(seconds, "batch"), axis=0)
     mine_ids = lax.dynamic_slice_in_dim(request_adapter_index, batch_row * requests, requests)
     my_owner = mine_ids // present
     positions = jnp.arange(requests, dtype=jnp.int32)
     earlier = (my_owner[:, None] == my_owner[None, :]) & (positions[None, :] < positions[:, None])
-    slot_code = my_owner * CAP + jnp.sum(earlier.astype(jnp.int32), axis=1)
-
-    every_query = lax.all_gather(queries, "mp", axis=0)
-    left = lengths - column * prefix_here
-    partial = attend(left, every_query, prefix_key_cache, prefix_value_cache)
+    distance = (batch_row - my_owner + batch_size) % batch_size
+    slot_code = distance * CAP + jnp.sum(earlier.astype(jnp.int32), axis=1)
+
+    every_query = jnp.stack(exchange([queries] * columns, "mp"), axis=0)
+    meta = jnp.concatenate([left, column.reshape(1)])
+    partial = attend(meta, every_query, prefix_key_cache, prefix_value_cache)
     got = lax.all_to_all(partial, "mp", split_axis=0, concat_axis=0, tiled=True)
     kv_group = (column * heads_here // group_size).reshape(1)
     attended = merge(
         kv_group, got, queries, tree_node_keys, tree_node_values, ancestors(parents)
     )
-    shares = project(slot_code, attended, down, output_projection_weight, columns)
+    shares = project(slot_code, attended, maps, output_projection_weight, columns)
     base = lax.psum_scatter(shares, "mp", scatter_dimension=0, tiled=False)
-    return finish(slot_code, base, up, requests)
+    return finish(slot_code, base, maps, rest, requests)
 
 
 def solution(mesh):

time: 167 us -> 131 us (0.78)
  blocking collectives: 51.3 us -> 0 us
  local copies, waits for them, and re-layouts: 3.89 us -> 17.1 us
  starting transfers between devices: 8.27 us -> 20.7 us
  waiting for transfers between devices: 52.2 us -> 40.6 us
  Pallas kernels: 35.2 us -> 32.4 us
  other arithmetic: 1.36 us -> 3.72 us
    all_to_all x1 -> x0, blocking collectives: 51.3 us -> none  [per_device(): lax.all_to_all(send_up, 'batch', split_axis=0, concat_axis=0, tiled=True)]
    ppermute x0 -> x9, waiting for transfers between devices: none -> 21.4 us  [exchange(): got.append(lax.ppermute(blocks[shift], axis, pairs))]
    all_to_all x1 -> x0, waiting for transfers between devices: 20.5 us -> none  [per_device(): lax.all_to_all(send_down, 'batch', split_axis=0, concat_axis=0, tiled=True)]
    all_gather x1 -> x0, waiting for transfers between devices: 20.5 us -> none  [per_device(): every_query = lax.all_gather(queries, 'mp', axis=0)]
    ppermute x0 -> x9, starting transfers between devices: none -> 17 us  [exchange(): got.append(lax.ppermute(blocks[shift], axis, pairs))]
    reduce_scatter x1, waiting for transfers between devices: 0.01 us -> 12.8 us  [per_device(): base = lax.psum_scatter(shares, 'mp', scatter_dimension=0, tiled=False)]
    unnamed x20 -> x41, local copies, waits for them, and re-layouts: 3.63 us -> 15.1 us
    all_to_all x1 -> x0, starting transfers between devices: 4.6 us -> none  [per_device(): lax.all_to_all(send_down, 'batch', split_axis=0, concat_axis=0, tiled=True)]
  transfers between devices with their start and end apart: 4 -> 11, of which waited for: 3 -> 5; matrix products, arithmetic and copies ran while one was open for 1% -> 8% of each run, Pallas kernels for 4% -> 14%
where the time goes in v2:
time: 131 us; the launch traced here: 130 us
  waiting for transfers between devices  40.6 us (31%)
  Pallas kernels  32.4 us (25%)
  starting transfers between devices  20.7 us (16%)
  local copies, waits for them, and re-layouts  17.1 us (13%)
  between operations  13.6 us (10%)
  other arithmetic  3.72 us (3%)
  matrix products  2.21 us (2%)
    ppermute x9, waiting for transfers between devices, exchange(): got.append(lax.ppermute(blocks[shift], axis, pairs))  21.4 us
    ppermute x9, starting transfers between devices, exchange(): got.append(lax.ppermute(blocks[shift], axis, pairs))  17 us
    pallas_call x1, Pallas kernels, attend(): pl.pallas_call(functools.partial(attend_kernel, blocks), grid_spec=pltpu....  15.6 us
    unnamed x41, local copies, waits for them, and re-layouts  15.1 us
    reduce_scatter x1, waiting for transfers between devices, per_device(): base = lax.psum_scatter(shares, 'mp', scatter_dimension=0, tiled=False)  12.8 us
    pallas_call x1, Pallas kernels, project(): pl.pallas_call(project_kernel, grid_spec=pltpu.PrefetchScalarGridSpec(num...  8.12 us
    all_to_all x1, waiting for transfers between devices, per_device(): got = lax.all_to_all(partial, 'mp', split_axis=0, concat_axis=0, tiled=True)  6.35 us
    pallas_call x1, Pallas kernels, merge(): pl.pallas_call(merge_kernel, grid_spec=pltpu.PrefetchScalarGridSpec(num_s...  3.79 us
  transfers between devices with their start and end apart: 11, of which 5 were waited for; matrix products, arithmetic and copies ran while one was open for 8% of the time, Pallas kernels for 14%

profile of v2, /device:TPU:0, one launch (start us, length us, event | category | flops | bytes accessed | tf_op | source)
XLA Modules:
  0.0 130.2 jit_solution(11196181285210763310)
XLA Ops:
  6.5 0.5 collective-permute-start
  7.0 2.5 %collective-permute-start.1 = (bf16[4,32,1024]{2,1,0:T(8,128)(2,1)}, bf16[4,32,1024]{2,1,0:T(8,128)(2,1)}, u32[]{:S(2)}, u32[]{:S(2)}) collective-permute-start(bf16[4,32,1024]{2,1,0:T(8,128)(2,1)} %q_ref.1), channel_id=1, source_target_pairs={{0,2},{1,3},{2,0},{3,1},{4,6},{5,7},{6,4},{7,5},{8,10},{9,11},{10,... | collective-permute-start | bytes 786440 | tf_op jit(solution)/shard_map/ppermute | solution.py:96
  9.5 1.4 %collective-permute-start.2 = (bf16[4,32,1024]{2,1,0:T(8,128)(2,1)}, bf16[4,32,1024]{2,1,0:T(8,128)(2,1)}, u32[]{:S(2)}, u32[]{:S(2)}) collective-permute-start(bf16[4,32,1024]{2,1,0:T(8,128)(2,1)} %q_ref.1), channel_id=1, source_target_pairs={{0,3},{1,0},{2,1},{3,2},{4,7},{5,4},{6,5},{7,6},{8,11},{9,8},{10,9... | collective-permute-start | bytes 786440 | tf_op jit(solution)/shard_map/ppermute | solution.py:96
  11.0 0.7 reshape.156
  11.8 0.2 reduce_window_sum.11
  12.0 0.1 select_reduce_fusion.1
  12.1 0.2 select_reduce_fusion
  12.5 0.7 broadcast_subtract_fusion.left_ref
  13.1 1.2 copy-done.2
  14.4 1.0 copy-done.5
  15.4 2.5 %pick.1 = (s32[4]{0:T(128)S(1)}, bf16[2,64,2048]{2,1,0:T(8,128)(2,1)S(1)}, bf16[2,64,2048]{2,1,0:T(8,128)(2,1)}, bf16[2,64,2048]{2,1,0:T(8,128)(2,1)}, bf16[2,64...) custom-call(s32[8]{0:T(128)S(1)} %reshape.157.picked_ref, ...), custom_call_target="tpu_custom_call" | custom-call | tf_op jit(solution)/shard_map/pick/pallas_call | solution.py:77
  17.9 0.7 copy-done.7
  18.6 0.8 copy-done.11
  19.4 0.7 copy-done.12
  20.1 0.7 copy-done.14
  20.8 0.7 copy-done.16
  21.5 1.6 %collective-permute-start.3 = (bf16[2,64,2048]{2,1,0:T(8,128)(2,1)}, bf16[2,64,2048]{2,1,0:T(8,128)(2,1)}, u32[]{:S(2)}, u32[]{:S(2)}) collective-permute-start(bf16[2,64,2048]{2,1,0:T(8,128)(2,1)} %get-tuple-element.16), channel_id=1, source_target_pairs={{0,4},{4,8},{8,12},{12,0},{1,5},{5,9},{9,13},{13,1},{2,6},{6,10},{... | collective-permute-start | bytes 1572872 | tf_op jit(solution)/shard_map/ppermute | solution.py:96
  23.0 2.6 %collective-permute-start.4 = (bf16[2,64,2048]{2,1,0:T(8,128)(2,1)}, bf16[2,64,2048]{2,1,0:T(8,128)(2,1)}, u32[]{:S(2)}, u32[]{:S(2)}) collective-permute-start(bf16[2,64,2048]{2,1,0:T(8,128)(2,1)} %get-tuple-element.17), channel_id=1, source_target_pairs={{0,8},{4,12},{8,0},{12,4},{1,9},{5,13},{9,1},{13,5},{2,10},{6,14},... | collective-permute-start | bytes 1572872 | tf_op jit(solution)/shard_map/ppermute | solution.py:96
  25.6 1.2 fusion.1
  26.8 0.3 fusion.3
  27.1 0.7 convolution_minimum_fusion.linked_ref
  27.9 0.7 and_select_fusion.2
  28.6 0.2 convert_reduce_fusion
  28.9 1.4 %collective-permute-start.5 = (bf16[2,64,2048]{2,1,0:T(8,128)(2,1)}, bf16[2,64,2048]{2,1,0:T(8,128)(2,1)}, u32[]{:S(2)}, u32[]{:S(2)}) collective-permute-start(bf16[2,64,2048]{2,1,0:T(8,128)(2,1)} %copy-done.11), channel_id=1, source_target_pairs={{0,12},{4,0},{8,4},{12,8},{1,13},{5,1},{9,5},{13,9},{2,14},{6,2},{... | collective-permute-start | bytes 1572872 | tf_op jit(solution)/shard_map/ppermute | solution.py:96
  30.3 1.2 pad_maximum_fusion.refs_0_
  31.6 15.6 %attend.1 = bf16[4,9,4,32,128]{4,3,2,1,0:T(8,128)(2,1)S(1)} custom-call(s32[5]{0:T(128)S(1)} %pad_add_fusion.meta_ref, bf16[4,4,32,1024]{3,2,1,0:T(8,128)(2,1)S(1)} %pad_maximum_fusion.refs_0_, bf16[4,1024,512]{2,1,0:T(8,128)(2,1)} %refs_1_.1, bf16[4,1024,512]{2,1,0:T(8,128)(2,1)} %refs_2_.1), custom_call_target="tpu_custom_call" | custom-call | flops 2147483648 | bytes 8388608 | tf_op jit(solution)/shard_map/attend/pallas_call | solution.py:148
  47.1 1.0 copy-done.1
  48.2 3.7 %all-to-all-start = ((bf16[4,9,4,32,128]{4,3,2,1,0:T(8,128)(2,1)}), bf16[4,9,4,32,128]{4,3,2,1,0:T(8,128)(2,1)S(1)}, u32[]{:S(2)}, u32[]{:S(2)}) async-start(bf16[4,9,4,32,128]{4,3,2,1,0:T(8,128)(2,1)} %copy-done.1), calls=%async_computation | async-start | bytes 2359296 | tf_op jit(solution)/shard_map/all_to_all | solution.py:350
  52.0 1.1 constant_dynamic-update-slice_fusion.2
  53.1 6.1 %collective-permute-done.4 = bf16[2,64,2048]{2,1,0:T(8,128)(2,1)} collective-permute-done((bf16[2,64,2048]{2,1,0:T(8,128)(2,1)}, bf16[2,64,2048]{2,1,0:T(8,128)(2,1)}, u32[]{:S(2)}, u32[]{:S(2)}) %collective-permute-start.4) | collective-permute-done | bytes 524320 | tf_op jit(solution)/shard_map/ppermute | solution.py:96
  59.2 1.1 constant_dynamic-update-slice_fusion.1
  60.2 1.1 constant_dynamic-update-slice_fusion.down_ref.first_ref
  61.3 6.4 %all-to-all-done.got_ref = bf16[4,9,4,32,128]{4,3,2,1,0:T(8,128)(2,1)S(1)} async-done(((bf16[4,9,4,32,128]{4,3,2,1,0:T(8,128)(2,1)}), bf16[4,9,4,32,128]{4,3,2,1,0:T(8,128)(2,1)S(1)}, u32[]{:S(2)}, u32[]{:S(2)}) %all-to-all-start) | async-done | bytes 1179680 | tf_op jit(solution)/shard_map/all_to_all | solution.py:350
  67.7 0.8 copy-done.6
  68.5 0.9 copy-done.9
  69.4 0.9 copy-done.10
  70.3 3.8 %merge.1.x_ref = bf16[4,32,1024]{2,1,0:T(8,128)(2,1)S(1)} custom-call(s32[1]{0:T(128)} %bitcast.kv_ref, bf16[4,9,4,32,128]{4,3,2,1,0:T(8,128)(2,1)S(1)} %all-to-all-done.got_ref, bf16[4,32,1024]{2,1,0:T(8,128)(2,1)S(1)} %copy-done.3, bf16[4,32,512]{2,1,0:T(8,128)(2,1)S(1)} %copy-done.9, bf16[4,32,512]{2,1,0:T(8,128)(2,1)S(1)} %copy-done.10, ...), custom_call_target="tpu_custom_call" | custom-call | tf_op jit(solution)/shard_map/merge/pallas_call | solution.py:211
  74.1 8.1 %project.1 = bf16[4,128,2176]{2,1,0:T(8,128)(2,1)S(1)} custom-call(s32[4]{0:T(128)S(1)} %fusion.17.slot_ref, bf16[4,32,1024]{2,1,0:T(8,128)(2,1)S(1)} %merge.1.x_ref, bf16[8,64,2048]{2,1,0:T(8,128)(2,1)S(1)} %constant_dynamic-update-slice_fusion.down_ref.first_ref, bf16[1024,8192]{1,0:T(8,128)(2,1)} %w_ref.1), custom_call_target="tpu_custom_call" | custom-call | tf_op jit(solution)/shard_map/project/pallas_call | solution.py:253
  82.3 1.4 %copy-done = bf16[4,128,2176]{2,1,0:T(8,128)(2,1)} copy-done((bf16[4,128,2176]{2,1,0:T(8,128)(2,1)}, bf16[4,128,2176]{2,1,0:T(8,128)(2,1)S(1)}, u32[]{:S(2)}) %copy-start) | copy-done | bytes 2228248
  83.7 0.9 copy-done.17
  84.6 4.3 %collective-permute-start.6 = (bf16[2,64,1024]{2,1,0:T(8,128)(2,1)S(1)}, bf16[2,64,1024]{2,1,0:T(8,128)(2,1)S(1)}, u32[]{:S(2)}, u32[]{:S(2)}) collective-permute-start(bf16[2,64,1024]{2,1,0:T(8,128)(2,1)S(1)} %copy-done.17), channel_id=1, source_target_pairs={{0,4},{4,8},{8,12},{12,0},{1,5},{5,9},{9,13},{13,1},{2,6},{6,10},{... | collective-permute-start | bytes 786440 | tf_op jit(solution)/shard_map/ppermute | solution.py:96
  88.9 2.7 %collective-permute-start.7 = (bf16[2,64,1024]{2,1,0:T(8,128)(2,1)S(1)}, bf16[2,64,1024]{2,1,0:T(8,128)(2,1)S(1)}, u32[]{:S(2)}, u32[]{:S(2)}) collective-permute-start(bf16[2,64,1024]{2,1,0:T(8,128)(2,1)S(1)} %copy-done.15), channel_id=1, source_target_pairs={{0,8},{4,12},{8,0},{12,4},{1,9},{5,13},{9,1},{13,5},{2,10},{6,14},... | collective-permute-start | bytes 786440 | tf_op jit(solution)/shard_map/ppermute | solution.py:96
  91.5 6.7 %collective-permute-done.6 = bf16[2,64,1024]{2,1,0:T(8,128)(2,1)S(1)} collective-permute-done((bf16[2,64,1024]{2,1,0:T(8,128)(2,1)S(1)}, bf16[2,64,1024]{2,1,0:T(8,128)(2,1)S(1)}, u32[]{:S(2)}, u32[]{:S(2)}) %collective-permute-start.6) | collective-permute-done | bytes 262176 | tf_op jit(solution)/shard_map/ppermute | solution.py:96
  98.3 8.6 %collective-permute-done.7 = bf16[2,64,1024]{2,1,0:T(8,128)(2,1)S(1)} collective-permute-done((bf16[2,64,1024]{2,1,0:T(8,128)(2,1)S(1)}, bf16[2,64,1024]{2,1,0:T(8,128)(2,1)S(1)}, u32[]{:S(2)}, u32[]{:S(2)}) %collective-permute-start.7) | collective-permute-done | bytes 262176 | tf_op jit(solution)/shard_map/ppermute | solution.py:96
  106.9 0.1 pad_maximum_fusion.1.second_ref
  107.1 12.8 %reduce-scatter.2.cloned.1.call-done = bf16[1,128,2176]{2,1,0:T(8,128)(2,1)} async-done(((bf16[4,128,2176]{2,1,0:T(8,128)(2,1)}), bf16[1,128,2176]{2,1,0:T(8,128)(2,1)}) %reduce-scatter.2.cloned.1.call-update) | async-done | bytes 557072 | tf_op jit(solution)/shard_map/reduce_scatter | solution.py:356
  119.9 1.1 copy-done.4
  120.9 2.4 %finish.1 = bf16[4,32,2048]{2,1,0:T(8,128)(2,1)} custom-call(s32[4]{0:T(128)S(1)} %fusion.17.slot_ref, bf16[128,2176]{1,0:T(8,128)(2,1)S(1)} %bitcast.12, bf16[8,64,2048]{2,1,0:T(8,128)(2,1)S(1)} %constant_dynamic-update-slice_fusion.down_ref.first_ref, bf16[8,64,1024]{2,1,0:T(8,128)(2,1)S(1)} %pad_maximum_fusion.1.second_ref), custom_call_target="tpu_custom_call" | custom-call | tf_op jit(solution)/shard_map/finish/pallas_call | solution.py:287
  (43 shorter events, 0.6 us)
Async XLA Ops:
  6.5 22.4 %collective-permute-start = (bf16[4,32,1024]{2,1,0:T(8,128)(2,1)}, bf16[4,32,1024]{2,1,0:T(8,128)(2,1)}, u32[]{:S(2)}, u32[]{:S(2)}) collective-permute-start(bf16[4,32,1024]{2,1,0:T(8,128)(2,1)} %q_ref.1), channel_id=1, source_target_pairs={{0,1},{1,2},{2,3},{3,0},{4,5},{5,6},{6,7},{7,4},{8,9},{9,10},{10,1... | collective-permute-start | bytes 786440 | tf_op jit(solution)/shard_map/ppermute | solution.py:96
  7.0 23.3 %collective-permute-start.1 = (bf16[4,32,1024]{2,1,0:T(8,128)(2,1)}, bf16[4,32,1024]{2,1,0:T(8,128)(2,1)}, u32[]{:S(2)}, u32[]{:S(2)}) collective-permute-start(bf16[4,32,1024]{2,1,0:T(8,128)(2,1)} %q_ref.1), channel_id=1, source_target_pairs={{0,2},{1,3},{2,0},{3,1},{4,6},{5,7},{6,4},{7,5},{8,10},{9,11},{10,... | collective-permute-start | bytes 786440 | tf_op jit(solution)/shard_map/ppermute | solution.py:96
  9.5 20.8 %collective-permute-start.2 = (bf16[4,32,1024]{2,1,0:T(8,128)(2,1)}, bf16[4,32,1024]{2,1,0:T(8,128)(2,1)}, u32[]{:S(2)}, u32[]{:S(2)}) collective-permute-start(bf16[4,32,1024]{2,1,0:T(8,128)(2,1)} %q_ref.1), channel_id=1, source_target_pairs={{0,3},{1,0},{2,1},{3,2},{4,7},{5,4},{6,5},{7,6},{8,11},{9,8},{10,9... | collective-permute-start | bytes 786440 | tf_op jit(solution)/shard_map/ppermute | solution.py:96
  13.1 1.2 copy-start.2
  14.4 1.0 copy-start.5
  15.4 14.9 %copy-start.3 = (bf16[4,32,1024]{2,1,0:T(8,128)(2,1)S(1)}, bf16[4,32,1024]{2,1,0:T(8,128)(2,1)}, u32[]{:S(2)}) copy-start(bf16[4,32,1024]{2,1,0:T(8,128)(2,1)} %q_ref.1) | copy-start | bytes 786436
  17.9 0.7 copy-start.7
  18.6 0.8 copy-start.11
  19.4 0.7 copy-start.12
  20.1 0.7 copy-start.14
  20.8 0.7 copy-start.16
  21.5 30.5 %collective-permute-start.3 = (bf16[2,64,2048]{2,1,0:T(8,128)(2,1)}, bf16[2,64,2048]{2,1,0:T(8,128)(2,1)}, u32[]{:S(2)}, u32[]{:S(2)}) collective-permute-start(bf16[2,64,2048]{2,1,0:T(8,128)(2,1)} %get-tuple-element.16), channel_id=1, source_target_pairs={{0,4},{4,8},{8,12},{12,0},{1,5},{5,9},{9,13},{13,1},{2,6},{6,10},{... | collective-permute-start | bytes 1572872 | tf_op jit(solution)/shard_map/ppermute | solution.py:96
  23.0 36.1 %collective-permute-start.4 = (bf16[2,64,2048]{2,1,0:T(8,128)(2,1)}, bf16[2,64,2048]{2,1,0:T(8,128)(2,1)}, u32[]{:S(2)}, u32[]{:S(2)}) collective-permute-start(bf16[2,64,2048]{2,1,0:T(8,128)(2,1)} %get-tuple-element.17), channel_id=1, source_target_pairs={{0,8},{4,12},{8,0},{12,4},{1,9},{5,13},{9,1},{13,5},{2,10},{6,14},... | collective-permute-start | bytes 1572872 | tf_op jit(solution)/shard_map/ppermute | solution.py:96
  28.9 31.3 %collective-permute-start.5 = (bf16[2,64,2048]{2,1,0:T(8,128)(2,1)}, bf16[2,64,2048]{2,1,0:T(8,128)(2,1)}, u32[]{:S(2)}, u32[]{:S(2)}) collective-permute-start(bf16[2,64,2048]{2,1,0:T(8,128)(2,1)} %copy-done.11), channel_id=1, source_target_pairs={{0,12},{4,0},{8,4},{12,8},{1,13},{5,1},{9,5},{13,9},{2,14},{6,2},{... | collective-permute-start | bytes 1572872 | tf_op jit(solution)/shard_map/ppermute | solution.py:96
  47.1 1.0 copy-start.1
  48.2 3.7 %copy-start.18 = (s32[16]{0:T(128)S(1)}, s32[16]{0:T(128)}, u32[]{:S(2)}) copy-start(s32[16]{0:T(128)} %param.18) | copy-start | bytes 196
  48.2 19.5 %all-to-all-start = ((bf16[4,9,4,32,128]{4,3,2,1,0:T(8,128)(2,1)}), bf16[4,9,4,32,128]{4,3,2,1,0:T(8,128)(2,1)S(1)}, u32[]{:S(2)}, u32[]{:S(2)}) async-start(bf16[4,9,4,32,128]{4,3,2,1,0:T(8,128)(2,1)} %copy-done.1), calls=%async_computation | async-start | bytes 2359296 | tf_op jit(solution)/shard_map/all_to_all | solution.py:350
  51.8 68.0 %reduce-scatter.2.cloned.1.call-start = ((), (), s32[]{:S(2)}) async-start(), calls=%async_computation.2 | async-start | bytes 2785280 | tf_op jit(solution)/shard_map/reduce_scatter | solution.py:356
  67.7 0.8 copy-start.6
  68.5 0.9 copy-start.9
  69.4 0.9 copy-start.10
  82.3 1.4 %copy-start = (bf16[4,128,2176]{2,1,0:T(8,128)(2,1)}, bf16[4,128,2176]{2,1,0:T(8,128)(2,1)S(1)}, u32[]{:S(2)}) copy-start(bf16[4,128,2176]{2,1,0:T(8,128)(2,1)S(1)} %project.1) | copy-start | bytes 6684676
  83.6 0.9 copy-start.17
  83.6 5.2 %copy-start.15 = (bf16[2,64,1024]{2,1,0:T(8,128)(2,1)S(1)}, bf16[2,64,1024]{2,1,0:T(8,128)(2,1)}, u32[]{:S(2)}) copy-start(bf16[2,64,1024]{2,1,0:T(8,128)(2,1)} %copy-done.14) | copy-start | bytes 786436
  83.6 7.9 %copy-start.13 = (bf16[2,64,1024]{2,1,0:T(8,128)(2,1)S(1)}, bf16[2,64,1024]{2,1,0:T(8,128)(2,1)}, u32[]{:S(2)}) copy-start(bf16[2,64,1024]{2,1,0:T(8,128)(2,1)} %copy-done.12) | copy-start | bytes 786436
  83.6 23.3 %copy-start.8 = (bf16[2,64,1024]{2,1,0:T(8,128)(2,1)S(1)}, bf16[2,64,1024]{2,1,0:T(8,128)(2,1)}, u32[]{:S(2)}) copy-start(bf16[2,64,1024]{2,1,0:T(8,128)(2,1)} %copy-done.7) | copy-start | bytes 786436
  84.6 13.7 %collective-permute-start.6 = (bf16[2,64,1024]{2,1,0:T(8,128)(2,1)S(1)}, bf16[2,64,1024]{2,1,0:T(8,128)(2,1)S(1)}, u32[]{:S(2)}, u32[]{:S(2)}) collective-permute-start(bf16[2,64,1024]{2,1,0:T(8,128)(2,1)S(1)} %copy-done.17), channel_id=1, source_target_pairs={{0,4},{4,8},{8,12},{12,0},{1,5},{5,9},{9,13},{13,1},{2,6},{6,10},{... | collective-permute-start | bytes 786440 | tf_op jit(solution)/shard_map/ppermute | solution.py:96
  88.9 18.1 %collective-permute-start.7 = (bf16[2,64,1024]{2,1,0:T(8,128)(2,1)S(1)}, bf16[2,64,1024]{2,1,0:T(8,128)(2,1)S(1)}, u32[]{:S(2)}, u32[]{:S(2)}) collective-permute-start(bf16[2,64,1024]{2,1,0:T(8,128)(2,1)S(1)} %copy-done.15), channel_id=1, source_target_pairs={{0,8},{4,12},{8,0},{12,4},{1,9},{5,13},{9,1},{13,5},{2,10},{6,14},... | collective-permute-start | bytes 786440 | tf_op jit(solution)/shard_map/ppermute | solution.py:96
  91.5 15.4 %collective-permute-start.8 = (bf16[2,64,1024]{2,1,0:T(8,128)(2,1)S(1)}, bf16[2,64,1024]{2,1,0:T(8,128)(2,1)S(1)}, u32[]{:S(2)}, u32[]{:S(2)}) collective-permute-start(bf16[2,64,1024]{2,1,0:T(8,128)(2,1)S(1)} %copy-done.13), channel_id=1, source_target_pairs={{0,12},{4,0},{8,4},{12,8},{1,13},{5,1},{9,5},{13,9},{2,14},{6,2},{... | collective-permute-start | bytes 786440 | tf_op jit(solution)/shard_map/ppermute | solution.py:96
  119.9 1.1 copy-start.4
Sparse Core Ops, SparseCore 0:
  83.8 36.0 reduce-scatter.1

commit v3 on v2

--- a/solution.py
+++ b/solution.py
@@ -228,23 +228,18 @@
     )(kv_group, got, queries, tree_keys, tree_values, linked)
 
 
-def project_kernel(slot_ref, x_ref, down_ref, w_ref, out_ref, shrunk_ref):
+def project_kernel(slot_ref, x_ref, down_ref, w_ref, out_ref):
     requests, nodes, width_here = x_ref.shape
     wide = w_ref.shape[1]
-
-    @pl.when(pl.program_id(0) == 0)
-    def _():
-        shrunk_ref[...] = jnp.zeros_like(shrunk_ref)
-        for r in range(requests):
-            part = dot(x_ref[r], down_ref[slot_ref[r]], CONTRACT_LAST)
-            shrunk_ref[r * nodes : (r + 1) * nodes, :ADAPTER_RANK] = part.astype(jnp.bfloat16)
-
     rows = x_ref[...].reshape(requests * nodes, width_here)
-    out_ref[0, :, :wide] = dot(rows, w_ref[...]).astype(jnp.bfloat16)
-    out_ref[0, :, wide:] = shrunk_ref[...]
-
-
-def project(slot_code, attended, maps, weight, columns):
+    out_ref[:, :wide] = dot(rows, w_ref[...]).astype(jnp.bfloat16)
+    out_ref[:, wide:] = jnp.zeros((requests * nodes, LANES), jnp.bfloat16)
+    for r in range(requests):
+        part = dot(x_ref[r], down_ref[slot_ref[r]], CONTRACT_LAST)
+        out_ref[r * nodes : (r + 1) * nodes, wide : wide + ADAPTER_RANK] = part.astype(jnp.bfloat16)
+
+
+def project(meta, attended, maps, weight, columns):
     requests, nodes, width_here = attended.shape
     slots = maps.shape[0]
     down_block = maps.shape[2] // width_here - 1
@@ -254,48 +249,62 @@
         project_kernel,
         grid_spec=pltpu.PrefetchScalarGridSpec(
             num_scalar_prefetch=1,
-            grid=(columns,),
+            grid=(1,),
             in_specs=[
-                pl.BlockSpec((requests, nodes, width_here), lambda c, s: (0, 0, 0)),
-                pl.BlockSpec((slots, ADAPTER_RANK, width_here), lambda c, s: (0, 0, down_block)),
-                pl.BlockSpec((width_here, wide), lambda c, s: (0, c)),
+                pl.BlockSpec((requests, nodes, width_here), lambda i, s: (0, 0, 0)),
+                pl.BlockSpec((slots, ADAPTER_RANK, width_here), lambda i, s: (0, 0, down_block)),
+                pl.BlockSpec((width_here, wide), lambda i, s: (0, s[requests])),
             ],
-            out_specs=pl.BlockSpec((1, rows, wide + LANES), lambda c, s: (c, 0, 0)),
-            scratch_shapes=[pltpu.VMEM((rows, LANES), jnp.bfloat16)],
-        ),
-        out_shape=jax.ShapeDtypeStruct((columns, rows, wide + LANES), jnp.bfloat16),
-        compiler_params=params(),
+            out_specs=pl.BlockSpec((rows, wide + LANES), lambda i, s: (0, 0)),
+        ),
+        out_shape=jax.ShapeDtypeStruct((rows, wide + LANES), jnp.bfloat16),
+        compiler_params=params(),
+        cost_estimate=pl.CostEstimate(
+            flops=2 * rows * width_here * wide,
+            bytes_accessed=2 * width_here * wide,
+            transcendentals=0,
+        ),
         name="project",
-    )(slot_code, attended, maps, weight)
-
-
-def raise_kernel(slot_ref, base_ref, first_ref, second_ref, out_ref):
+    )(meta, attended, maps, weight)
+
+
+def raise_kernel(slot_ref, first_ref, second_ref, *refs):
+    share_refs, out_ref = refs[:-1], refs[-1]
     wide = out_ref.shape[2]
     half = wide // 2
-    shrunk = base_ref[:, wide : wide + ADAPTER_RANK]
+
+    def added(start, size):
+        total = share_refs[0][:, start : start + size].astype(jnp.float32)
+        for share_ref in share_refs[1:]:
+            total = total + share_ref[:, start : start + size].astype(jnp.float32)
+        return total
+
+    shrunk = added(wide, LANES)[:, :ADAPTER_RANK].astype(jnp.bfloat16)
     for at, up_ref in ((0, first_ref), (half, second_ref)):
         raised = dot(shrunk, up_ref[0])
-        projected = base_ref[:, at : at + half].astype(jnp.float32)
-        out_ref[0, :, at : at + half] = (projected + ADAPTER_SCALE * raised).astype(jnp.bfloat16)
-
-
-def finish(slot_code, base, maps, rest, requests):
-    rows, wider = base.shape
+        out_ref[0, :, at : at + half] = (added(at, half) + ADAPTER_SCALE * raised).astype(
+            jnp.bfloat16
+        )
+
+
+def finish(slot_code, shares, maps, rest, requests):
+    rows, wider = shares[0].shape
     wide = wider - LANES
     nodes = rows // requests
     up_spec = pl.BlockSpec((1, ADAPTER_RANK, wide // 2), lambda r, s: (s[r], 0, 0))
+    share_spec = pl.BlockSpec((nodes, wider), lambda r, s: (r, 0))
     return pl.pallas_call(
         raise_kernel,
         grid_spec=pltpu.PrefetchScalarGridSpec(
             num_scalar_prefetch=1,
             grid=(requests,),
-            in_specs=[pl.BlockSpec((nodes, wider), lambda r, s: (r, 0)), up_spec, up_spec],
+            in_specs=[up_spec, up_spec] + [share_spec] * len(shares),
             out_specs=pl.BlockSpec((1, nodes, wide), lambda r, s: (r, 0, 0)),
         ),
         out_shape=jax.ShapeDtypeStruct((requests, nodes, wide), jnp.bfloat16),
         compiler_params=params(),
         name="finish",
-    )(slot_code, base, maps, rest)
+    )(slot_code, maps, rest, *shares)
 
 
 def per_device(
@@ -352,9 +361,12 @@
     attended = merge(
         kv_group, got, queries, tree_node_keys, tree_node_values, ancestors(parents)
     )
-    shares = project(slot_code, attended, maps, output_projection_weight, columns)
-    base = lax.psum_scatter(shares, "mp", scatter_dimension=0, tiled=False)
-    return finish(slot_code, base, maps, rest, requests)
+    shares = []
+    for shift in range(columns):
+        target_column = ((column + shift) % columns).reshape(1)
+        project_meta = jnp.concatenate([slot_code, target_column])
+        shares.append(project(project_meta, attended, maps, output_projection_weight, columns))
+    return finish(slot_code, exchange(shares, "mp"), maps, rest, requests)
 
 
 def solution(mesh):

time: 131 us -> 115 us (0.88)
  the two profiles are of different devices: /device:TPU:0 before, /device:TPU:27 now
where the time goes in v3:
time: 115 us; the launch traced here: 114 us
  Pallas kernels  38.8 us (34%)
  waiting for transfers between devices  29.6 us (26%)
  starting transfers between devices  23.4 us (20%)
  local copies, waits for them, and re-layouts  14.3 us (12%)
  other arithmetic  5.26 us (5%)
  matrix products  2.22 us (2%)
    ppermute x12, waiting for transfers between devices, exchange(): got.append(lax.ppermute(blocks[shift], axis, pairs))  29.6 us
    ppermute x12, starting transfers between devices, exchange(): got.append(lax.ppermute(blocks[shift], axis, pairs))  17.2 us
    pallas_call x1, Pallas kernels, attend(): pl.pallas_call(functools.partial(attend_kernel, blocks), grid_spec=pltpu....  15.6 us
    pallas_call x4, Pallas kernels, project(): pl.pallas_call(project_kernel, grid_spec=pltpu.PrefetchScalarGridSpec(num...  14.5 us
    unnamed x37, local copies, waits for them, and re-layouts  12.3 us
    all_to_all x1, starting transfers between devices, per_device(): got = lax.all_to_all(partial, 'mp', split_axis=0, concat_axis=0, tiled=True)  6.18 us
    pallas_call x1, Pallas kernels, merge(): pl.pallas_call(merge_kernel, grid_spec=pltpu.PrefetchScalarGridSpec(num_s...  3.79 us
    pallas_call x1, Pallas kernels, finish(): pl.pallas_call(raise_kernel, grid_spec=pltpu.PrefetchScalarGridSpec(num_s...  2.46 us
  transfers between devices with their start and end apart: 13, of which 2 were waited for; matrix products, arithmetic and copies ran while one was open for 10% of the time, Pallas kernels for 32%

profile of v3, /device:TPU:27, one launch (start us, length us, event | category | flops | bytes accessed | tf_op | source)
XLA Modules:
  0.0 113.8 jit_solution(172252062156564785)
XLA Ops:
  0.0 1.8 %collective-permute-start.6 = (bf16[4,32,1024]{2,1,0:T(8,128)(2,1)}, bf16[4,32,1024]{2,1,0:T(8,128)(2,1)}, u32[]{:S(2)}, u32[]{:S(2)}) collective-permute-start(bf16[4,32,1024]{2,1,0:T(8,128)(2,1)} %q_ref.1), channel_id=1, source_target_pairs={{0,1},{1,2},{2,3},{3,0},{4,5},{5,6},{6,7},{7,4},{8,9},{9,10},{10,1... | collective-permute-start | bytes 786440 | tf_op jit(solution)/shard_map/ppermute | solution.py:96
  1.8 0.2 collective-permute-start.7
  2.0 0.2 collective-permute-start.8
  2.2 0.7 reshape.167
  3.1 0.2 reduce_window_sum.11
  3.4 0.2 select_reduce_fusion
  3.7 0.7 broadcast_subtract_fusion.left_ref
  4.4 1.2 %copy-done.1 = bf16[4,64,2048]{2,1,0:T(8,128)(2,1)S(1)} copy-done((bf16[4,64,2048]{2,1,0:T(8,128)(2,1)S(1)}, bf16[4,64,2048]{2,1,0:T(8,128)(2,1)}, u32[]{:S(2)}) %copy-start.1) | copy-done | bytes 1048600
  5.6 1.0 copy-done.3
  6.7 2.4 %pick.1 = (s32[4]{0:T(128)S(1)}, bf16[2,64,2048]{2,1,0:T(8,128)(2,1)S(1)}, bf16[2,64,2048]{2,1,0:T(8,128)(2,1)}, bf16[2,64,2048]{2,1,0:T(8,128)(2,1)}, bf16[2,64...) custom-call(s32[8]{0:T(128)S(1)} %reshape.168.picked_ref, ...), custom_call_target="tpu_custom_call" | custom-call | tf_op jit(solution)/shard_map/pick/pallas_call | solution.py:77
  9.1 0.7 copy-done.5
  9.8 0.8 copy-done.10
  10.6 0.7 copy-done.11
  11.3 0.7 copy-done.13
  12.0 0.7 copy-done.15
  12.8 1.3 %collective-permute-start.1 = (bf16[2,64,2048]{2,1,0:T(8,128)(2,1)}, bf16[2,64,2048]{2,1,0:T(8,128)(2,1)}, u32[]{:S(2)}, u32[]{:S(2)}) collective-permute-start(bf16[2,64,2048]{2,1,0:T(8,128)(2,1)} %get-tuple-element.16), channel_id=1, source_target_pairs={{0,8},{4,12},{8,0},{12,4},{1,9},{5,13},{9,1},{13,5},{2,10},{6,14},... | collective-permute-start | bytes 1572872 | tf_op jit(solution)/shard_map/ppermute | solution.py:96
  14.1 1.2 %fusion.1 = bf16[4,32,32]{2,1,0:T(8,128)(2,1)S(1)} fusion(s32[4,32]{1,0:T(4,128)} %param.17, f32[32,32]{1,0:T(8,128)S(1)} %fusion.11), kind=kOutput, calls=%fused_computation.6 | convolution fusion | flops 561152 | bytes 12800 | tf_op jit(solution)/shard_map/rnm,rmk->rnk/dot_general | solution.py:41
  15.3 0.3 fusion.3
  15.6 0.8 convolution_minimum_fusion.linked_ref
  16.3 0.7 and_select_fusion.2
  17.1 0.2 convert_reduce_fusion
  17.4 0.2 collective-permute-start.2
  17.6 3.1 %collective-permute-start.3 = (bf16[2,64,1024]{2,1,0:T(8,128)(2,1)}, bf16[2,64,1024]{2,1,0:T(8,128)(2,1)}, u32[]{:S(2)}, u32[]{:S(2)}) collective-permute-start(bf16[2,64,1024]{2,1,0:T(8,128)(2,1)} %copy-done.15), channel_id=1, source_target_pairs={{0,4},{4,8},{8,12},{12,0},{1,5},{5,9},{9,13},{13,1},{2,6},{6,10},{... | collective-permute-start | bytes 786440 | tf_op jit(solution)/shard_map/ppermute | solution.py:96
  20.7 1.2 %pad_maximum_fusion.1.refs_0_ = bf16[4,4,32,1024]{3,2,1,0:T(8,128)(2,1)S(1)} fusion(bf16[1,4,32,1024]{3,2,1,0:T(8,128)(2,1)} %bitcast.6, bf16[1,4,32,1024]{3,2,1,0:T(8,128)(2,1)} %bitcast.5, bf16[1,4,32,1024]{3,2,1,0:T(8,128)(2,1)} %bitcast.4, bf16[1,4,32,1024]{3,2,1,0:T(8,128)(2,1)S(1)} %bitcast.14), kind=kLoop, calls=%fused_computation.10 | loop fusion | flops 1572864 | bytes 2097152 | tf_op jit(solution)/shard_map/stack | solution.py:356
  22.0 15.6 %attend.1 = bf16[4,9,4,32,128]{4,3,2,1,0:T(8,128)(2,1)S(1)} custom-call(s32[5]{0:T(128)S(1)} %pad_add_fusion.1.meta_ref, bf16[4,4,32,1024]{3,2,1,0:T(8,128)(2,1)S(1)} %pad_maximum_fusion.1.refs_0_, bf16[4,1024,512]{2,1,0:T(8,128)(2,1)} %refs_1_.1, bf16[4,1024,512]{2,1,0:T(8,128)(2,1)} %refs_2_.1), custom_call_target="tpu_custom_call" | custom-call | flops 2147483648 | bytes 8388608 | tf_op jit(solution)/shard_map/attend/pallas_call | solution.py:148
  37.5 1.0 copy-done
  38.6 6.2 %all-to-all-start = ((bf16[4,9,4,32,128]{4,3,2,1,0:T(8,128)(2,1)}), bf16[4,9,4,32,128]{4,3,2,1,0:T(8,128)(2,1)S(1)}, u32[]{:S(2)}, u32[]{:S(2)}) async-start(bf16[4,9,4,32,128]{4,3,2,1,0:T(8,128)(2,1)} %copy-done), calls=%async_computation | async-start | bytes 2359296 | tf_op jit(solution)/shard_map/all_to_all | solution.py:359
  44.9 0.6 pad_add_fusion.4
  45.5 1.1 constant_dynamic-update-slice_fusion.2
  46.5 12.1 %collective-permute-done.1 = bf16[2,64,2048]{2,1,0:T(8,128)(2,1)} collective-permute-done((bf16[2,64,2048]{2,1,0:T(8,128)(2,1)}, bf16[2,64,2048]{2,1,0:T(8,128)(2,1)}, u32[]{:S(2)}, u32[]{:S(2)}) %collective-permute-start.1) | collective-permute-done | bytes 524320 | tf_op jit(solution)/shard_map/ppermute | solution.py:96
  58.6 1.1 constant_dynamic-update-slice_fusion.1
  59.7 1.1 constant_dynamic-update-slice_fusion.down_ref.first_ref
  60.9 0.8 copy-done.4
  61.7 0.9 copy-done.7
  62.6 0.9 copy-done.8
  63.5 3.8 %merge.1.x_ref = bf16[4,32,1024]{2,1,0:T(8,128)(2,1)S(1)} custom-call(s32[1]{0:T(128)} %bitcast.1.kv_ref, bf16[4,9,4,32,128]{4,3,2,1,0:T(8,128)(2,1)S(1)} %all-to-all-done.got_ref, bf16[4,32,1024]{2,1,0:T(8,128)(2,1)S(1)} %copy-done.2, bf16[4,32,512]{2,1,0:T(8,128)(2,1)S(1)} %copy-done.7, bf16[4,32,512]{2,1,0:T(8,128)(2,1)S(1)} %copy-done.8, ...), custom_call_target="tpu_custom_call" | custom-call | tf_op jit(solution)/shard_map/merge/pallas_call | solution.py:211
  67.3 0.6 copy-done.9
  67.9 3.6 %project.6 = bf16[128,2176]{1,0:T(8,128)(2,1)S(1)} custom-call(s32[5]{0:T(128)S(1)} %copy-done.9, bf16[4,32,1024]{2,1,0:T(8,128)(2,1)S(1)} %merge.1.x_ref, bf16[8,64,2048]{2,1,0:T(8,128)(2,1)S(1)} %constant_dynamic-update-slice_fusion.down_ref.first_ref, bf16[1024,8192]{1,0:T(8,128)(2,1)} %w_ref.7), custom_call_target="tpu_custom_call" | custom-call | flops 536870912 | bytes 4194304 | tf_op jit(solution)/shard_map/project/pallas_call | solution.py:248
  71.5 1.9 %collective-permute-start.10 = (bf16[128,2176]{1,0:T(8,128)(2,1)S(1)}, bf16[128,2176]{1,0:T(8,128)(2,1)S(1)}, u32[]{:S(2)}, u32[]{:S(2)}) collective-permute-start(bf16[128,2176]{1,0:T(8,128)(2,1)S(1)} %project.6), channel_id=1, source_target_pairs={{0,2},{1,3},{2,0},{3,1},{4,6},{5,7},{6,4},{7,5},{8,10},{9,11},{10,... | collective-permute-start | bytes 1671176 | tf_op jit(solution)/shard_map/ppermute | solution.py:96
  73.5 3.6 %project.7 = bf16[128,2176]{1,0:T(8,128)(2,1)S(1)} custom-call(s32[5]{0:T(128)S(1)} %get-tuple-element.25.slot_ref, bf16[4,32,1024]{2,1,0:T(8,128)(2,1)S(1)} %merge.1.x_ref, bf16[8,64,2048]{2,1,0:T(8,128)(2,1)S(1)} %constant_dynamic-update-slice_fusion.down_ref.first_ref, bf16[1024,8192]{1,0:T(8,128)(2,1)} %w_ref.7), custom_call_target="tpu_custom_call" | custom-call | flops 536870912 | bytes 4194304 | tf_op jit(solution)/shard_map/project/pallas_call | solution.py:248
  77.1 2.9 %collective-permute-start.11 = (bf16[128,2176]{1,0:T(8,128)(2,1)S(1)}, bf16[128,2176]{1,0:T(8,128)(2,1)S(1)}, u32[]{:S(2)}, u32[]{:S(2)}) collective-permute-start(bf16[128,2176]{1,0:T(8,128)(2,1)S(1)} %project.7), channel_id=1, source_target_pairs={{0,3},{1,0},{2,1},{3,2},{4,7},{5,4},{6,5},{7,6},{8,11},{9,8},{10,9... | collective-permute-start | bytes 1671176 | tf_op jit(solution)/shard_map/ppermute | solution.py:96
  80.0 3.6 %project.5 = bf16[128,2176]{1,0:T(8,128)(2,1)S(1)} custom-call(s32[5]{0:T(128)S(1)} %get-tuple-element.26.slot_ref, bf16[4,32,1024]{2,1,0:T(8,128)(2,1)S(1)} %merge.1.x_ref, bf16[8,64,2048]{2,1,0:T(8,128)(2,1)S(1)} %constant_dynamic-update-slice_fusion.down_ref.first_ref, bf16[1024,8192]{1,0:T(8,128)(2,1)} %w_ref.7), custom_call_target="tpu_custom_call" | custom-call | flops 536870912 | bytes 4194304 | tf_op jit(solution)/shard_map/project/pallas_call | solution.py:248
  83.6 1.2 %collective-permute-start.9 = (bf16[128,2176]{1,0:T(8,128)(2,1)S(1)}, bf16[128,2176]{1,0:T(8,128)(2,1)S(1)}, u32[]{:S(2)}, u32[]{:S(2)}) collective-permute-start(bf16[128,2176]{1,0:T(8,128)(2,1)S(1)} %project.5), channel_id=1, source_target_pairs={{0,1},{1,2},{2,3},{3,0},{4,5},{5,6},{6,7},{7,4},{8,9},{9,10},{10,1... | collective-permute-start | bytes 1671176 | tf_op jit(solution)/shard_map/ppermute | solution.py:96
  84.8 4.3 %collective-permute-start.4 = (bf16[2,64,1024]{2,1,0:T(8,128)(2,1)S(1)}, bf16[2,64,1024]{2,1,0:T(8,128)(2,1)S(1)}, u32[]{:S(2)}, u32[]{:S(2)}) collective-permute-start(bf16[2,64,1024]{2,1,0:T(8,128)(2,1)S(1)} %copy-done.14), channel_id=1, source_target_pairs={{0,8},{4,12},{8,0},{12,4},{1,9},{5,13},{9,1},{13,5},{2,10},{6,14},... | collective-permute-start | bytes 786440 | tf_op jit(solution)/shard_map/ppermute | solution.py:96
  89.1 17.5 %collective-permute-done.4 = bf16[2,64,1024]{2,1,0:T(8,128)(2,1)S(1)} collective-permute-done((bf16[2,64,1024]{2,1,0:T(8,128)(2,1)S(1)}, bf16[2,64,1024]{2,1,0:T(8,128)(2,1)S(1)}, u32[]{:S(2)}, u32[]{:S(2)}) %collective-permute-start.4) | collective-permute-done | bytes 262176 | tf_op jit(solution)/shard_map/ppermute | solution.py:96
  106.6 1.1 pad_maximum_fusion.second_ref
  107.7 3.6 %project.4.refs_0_ = bf16[128,2176]{1,0:T(8,128)(2,1)S(1)} custom-call(s32[5]{0:T(128)S(1)} %get-tuple-element.28.slot_ref, bf16[4,32,1024]{2,1,0:T(8,128)(2,1)S(1)} %merge.1.x_ref, bf16[8,64,2048]{2,1,0:T(8,128)(2,1)S(1)} %constant_dynamic-update-slice_fusion.down_ref.first_ref, bf16[1024,8192]{1,0:T(8,128)(2,1)} %w_ref.7), custom_call_target="tpu_custom_call" | custom-call | flops 536870912 | bytes 4194304 | tf_op jit(solution)/shard_map/project/pallas_call | solution.py:248
  111.4 2.5 %finish.1 = bf16[4,32,2048]{2,1,0:T(8,128)(2,1)} custom-call(s32[4]{0:T(128)S(1)} %fusion.17.slot_ref, bf16[8,64,2048]{2,1,0:T(8,128)(2,1)S(1)} %constant_dynamic-update-slice_fusion.down_ref.first_ref, bf16[8,64,1024]{2,1,0:T(8,128)(2,1)S(1)} %pad_maximum_fusion.second_ref, bf16[128,2176]{1,0:T(8,128)(2,1)S(1)} %project.4.refs_0_, ...), custom_call_target="tpu_custom_call" | custom-call | tf_op jit(solution)/shard_map/finish/pallas_call | solution.py:296
  (46 shorter events, 0.7 us)
Async XLA Ops:
  0.0 17.4 %collective-permute-start.6 = (bf16[4,32,1024]{2,1,0:T(8,128)(2,1)}, bf16[4,32,1024]{2,1,0:T(8,128)(2,1)}, u32[]{:S(2)}, u32[]{:S(2)}) collective-permute-start(bf16[4,32,1024]{2,1,0:T(8,128)(2,1)} %q_ref.1), channel_id=1, source_target_pairs={{0,1},{1,2},{2,3},{3,0},{4,5},{5,6},{6,7},{7,4},{8,9},{9,10},{10,1... | collective-permute-start | bytes 786440 | tf_op jit(solution)/shard_map/ppermute | solution.py:96
  1.8 15.8 %collective-permute-start.7 = (bf16[4,32,1024]{2,1,0:T(8,128)(2,1)}, bf16[4,32,1024]{2,1,0:T(8,128)(2,1)}, u32[]{:S(2)}, u32[]{:S(2)}) collective-permute-start(bf16[4,32,1024]{2,1,0:T(8,128)(2,1)} %q_ref.1), channel_id=1, source_target_pairs={{0,2},{1,3},{2,0},{3,1},{4,6},{5,7},{6,4},{7,5},{8,10},{9,11},{10,... | collective-permute-start | bytes 786440 | tf_op jit(solution)/shard_map/ppermute | solution.py:96
  2.0 18.7 %collective-permute-start.8 = (bf16[4,32,1024]{2,1,0:T(8,128)(2,1)}, bf16[4,32,1024]{2,1,0:T(8,128)(2,1)}, u32[]{:S(2)}, u32[]{:S(2)}) collective-permute-start(bf16[4,32,1024]{2,1,0:T(8,128)(2,1)} %q_ref.1), channel_id=1, source_target_pairs={{0,3},{1,0},{2,1},{3,2},{4,7},{5,4},{6,5},{7,6},{8,11},{9,8},{10,9... | collective-permute-start | bytes 786440 | tf_op jit(solution)/shard_map/ppermute | solution.py:96
  4.4 1.2 %copy-start.1 = (bf16[4,64,2048]{2,1,0:T(8,128)(2,1)S(1)}, bf16[4,64,2048]{2,1,0:T(8,128)(2,1)}, u32[]{:S(2)}) copy-start(bf16[4,64,2048]{2,1,0:T(8,128)(2,1)} %up_ref.1) | copy-start | bytes 3145732
  5.6 1.0 copy-start.3
  6.7 14.0 %copy-start.2 = (bf16[4,32,1024]{2,1,0:T(8,128)(2,1)S(1)}, bf16[4,32,1024]{2,1,0:T(8,128)(2,1)}, u32[]{:S(2)}) copy-start(bf16[4,32,1024]{2,1,0:T(8,128)(2,1)} %q_ref.1) | copy-start | bytes 786436
  9.1 0.7 copy-start.5
  9.8 0.8 copy-start.10
  10.6 0.7 copy-start.11
  11.3 0.7 copy-start.13
  12.0 0.7 copy-start.15
  12.7 32.7 %collective-permute-start = (bf16[2,64,2048]{2,1,0:T(8,128)(2,1)}, bf16[2,64,2048]{2,1,0:T(8,128)(2,1)}, u32[]{:S(2)}, u32[]{:S(2)}) collective-permute-start(bf16[2,64,2048]{2,1,0:T(8,128)(2,1)} %get-tuple-element.15), channel_id=1, source_target_pairs={{0,4},{4,8},{8,12},{12,0},{1,5},{5,9},{9,13},{13,1},{2,6},{6,10},{... | collective-permute-start | bytes 1572872 | tf_op jit(solution)/shard_map/ppermute | solution.py:96
  12.8 45.9 %collective-permute-start.1 = (bf16[2,64,2048]{2,1,0:T(8,128)(2,1)}, bf16[2,64,2048]{2,1,0:T(8,128)(2,1)}, u32[]{:S(2)}, u32[]{:S(2)}) collective-permute-start(bf16[2,64,2048]{2,1,0:T(8,128)(2,1)} %get-tuple-element.16), channel_id=1, source_target_pairs={{0,8},{4,12},{8,0},{12,4},{1,9},{5,13},{9,1},{13,5},{2,10},{6,14},... | collective-permute-start | bytes 1572872 | tf_op jit(solution)/shard_map/ppermute | solution.py:96
  17.4 42.3 %collective-permute-start.2 = (bf16[2,64,2048]{2,1,0:T(8,128)(2,1)}, bf16[2,64,2048]{2,1,0:T(8,128)(2,1)}, u32[]{:S(2)}, u32[]{:S(2)}) collective-permute-start(bf16[2,64,2048]{2,1,0:T(8,128)(2,1)} %copy-done.10), channel_id=1, source_target_pairs={{0,12},{4,0},{8,4},{12,8},{1,13},{5,1},{9,5},{13,9},{2,14},{6,2},{... | collective-permute-start | bytes 1572872 | tf_op jit(solution)/shard_map/ppermute | solution.py:96
  17.6 71.5 %collective-permute-start.3 = (bf16[2,64,1024]{2,1,0:T(8,128)(2,1)}, bf16[2,64,1024]{2,1,0:T(8,128)(2,1)}, u32[]{:S(2)}, u32[]{:S(2)}) collective-permute-start(bf16[2,64,1024]{2,1,0:T(8,128)(2,1)} %copy-done.15), channel_id=1, source_target_pairs={{0,4},{4,8},{8,12},{12,0},{1,5},{5,9},{9,13},{13,1},{2,6},{6,10},{... | collective-permute-start | bytes 786440 | tf_op jit(solution)/shard_map/ppermute | solution.py:96
  37.5 1.0 copy-start
  38.6 6.2 %copy-start.16 = (s32[16]{0:T(128)S(1)}, s32[16]{0:T(128)}, u32[]{:S(2)}) copy-start(s32[16]{0:T(128)} %param.18) | copy-start | bytes 196
  38.6 22.3 %all-to-all-start = ((bf16[4,9,4,32,128]{4,3,2,1,0:T(8,128)(2,1)}), bf16[4,9,4,32,128]{4,3,2,1,0:T(8,128)(2,1)S(1)}, u32[]{:S(2)}, u32[]{:S(2)}) async-start(bf16[4,9,4,32,128]{4,3,2,1,0:T(8,128)(2,1)} %copy-done), calls=%async_computation | async-start | bytes 2359296 | tf_op jit(solution)/shard_map/all_to_all | solution.py:359
  60.8 0.8 copy-start.4
  61.7 0.9 copy-start.7
  62.6 0.9 copy-start.8
  67.3 0.6 copy-start.9
  71.5 39.8 %collective-permute-start.10 = (bf16[128,2176]{1,0:T(8,128)(2,1)S(1)}, bf16[128,2176]{1,0:T(8,128)(2,1)S(1)}, u32[]{:S(2)}, u32[]{:S(2)}) collective-permute-start(bf16[128,2176]{1,0:T(8,128)(2,1)S(1)} %project.6), channel_id=1, source_target_pairs={{0,2},{1,3},{2,0},{3,1},{4,6},{5,7},{6,4},{7,5},{8,10},{9,11},{10,... | collective-permute-start | bytes 1671176 | tf_op jit(solution)/shard_map/ppermute | solution.py:96
  77.1 34.3 %collective-permute-start.11 = (bf16[128,2176]{1,0:T(8,128)(2,1)S(1)}, bf16[128,2176]{1,0:T(8,128)(2,1)S(1)}, u32[]{:S(2)}, u32[]{:S(2)}) collective-permute-start(bf16[128,2176]{1,0:T(8,128)(2,1)S(1)} %project.7), channel_id=1, source_target_pairs={{0,3},{1,0},{2,1},{3,2},{4,7},{5,4},{6,5},{7,6},{8,11},{9,8},{10,9... | collective-permute-start | bytes 1671176 | tf_op jit(solution)/shard_map/ppermute | solution.py:96
  80.0 4.9 %copy-start.14 = (bf16[2,64,1024]{2,1,0:T(8,128)(2,1)S(1)}, bf16[2,64,1024]{2,1,0:T(8,128)(2,1)}, u32[]{:S(2)}) copy-start(bf16[2,64,1024]{2,1,0:T(8,128)(2,1)} %copy-done.13) | copy-start | bytes 786436
  80.0 9.1 %copy-start.12 = (bf16[2,64,1024]{2,1,0:T(8,128)(2,1)S(1)}, bf16[2,64,1024]{2,1,0:T(8,128)(2,1)}, u32[]{:S(2)}) copy-start(bf16[2,64,1024]{2,1,0:T(8,128)(2,1)} %copy-done.11) | copy-start | bytes 786436
  80.0 26.6 %copy-start.6 = (bf16[2,64,1024]{2,1,0:T(8,128)(2,1)S(1)}, bf16[2,64,1024]{2,1,0:T(8,128)(2,1)}, u32[]{:S(2)}) copy-start(bf16[2,64,1024]{2,1,0:T(8,128)(2,1)} %copy-done.5) | copy-start | bytes 786436
  83.6 27.8 %collective-permute-start.9 = (bf16[128,2176]{1,0:T(8,128)(2,1)S(1)}, bf16[128,2176]{1,0:T(8,128)(2,1)S(1)}, u32[]{:S(2)}, u32[]{:S(2)}) collective-permute-start(bf16[128,2176]{1,0:T(8,128)(2,1)S(1)} %project.5), channel_id=1, source_target_pairs={{0,1},{1,2},{2,3},{3,0},{4,5},{5,6},{6,7},{7,4},{8,9},{9,10},{10,1... | collective-permute-start | bytes 1671176 | tf_op jit(solution)/shard_map/ppermute | solution.py:96
  84.8 21.8 %collective-permute-start.4 = (bf16[2,64,1024]{2,1,0:T(8,128)(2,1)S(1)}, bf16[2,64,1024]{2,1,0:T(8,128)(2,1)S(1)}, u32[]{:S(2)}, u32[]{:S(2)}) collective-permute-start(bf16[2,64,1024]{2,1,0:T(8,128)(2,1)S(1)} %copy-done.14), channel_id=1, source_target_pairs={{0,8},{4,12},{8,0},{12,4},{1,9},{5,13},{9,1},{13,5},{2,10},{6,14},... | collective-permute-start | bytes 786440 | tf_op jit(solution)/shard_map/ppermute | solution.py:96
  89.1 17.5 %collective-permute-start.5 = (bf16[2,64,1024]{2,1,0:T(8,128)(2,1)S(1)}, bf16[2,64,1024]{2,1,0:T(8,128)(2,1)S(1)}, u32[]{:S(2)}, u32[]{:S(2)}) collective-permute-start(bf16[2,64,1024]{2,1,0:T(8,128)(2,1)S(1)} %copy-done.12), channel_id=1, source_target_pairs={{0,12},{4,0},{8,4},{12,8},{1,13},{5,1},{9,5},{13,9},{2,14},{6,2},{... | collective-permute-start | bytes 786440 | tf_op jit(solution)/shard_map/ppermute | solution.py:96

commit v4 on v3

--- a/solution.py
+++ b/solution.py
@@ -99,8 +99,9 @@
 
 def attend_kernel(blocks, meta_ref, *refs):
     q_refs = refs[:blocks]
-    k_ref, v_ref, out_ref = refs[blocks:]
-    _, _, nodes, width_here = q_refs[0].shape
+    k_ref, v_ref = refs[blocks : blocks + 2]
+    out_refs = refs[blocks + 2 :]
+    _, nodes, width_here = q_refs[0].shape
     heads_here = width_here // HEAD_WIDTH
     request = pl.program_id(0)
     positions = k_ref.shape[1]
@@ -108,7 +109,7 @@
     rows = []
     for block in range(blocks):
         for head in range(heads_here):
-            rows.append(q_refs[block][0, 0, :, head * HEAD_WIDTH : (head + 1) * HEAD_WIDTH])
+            rows.append(q_refs[block][0, :, head * HEAD_WIDTH : (head + 1) * HEAD_WIDTH])
     query = jnp.concatenate(rows, axis=0)
     scores = dot(query, k_ref[0], CONTRACT_LAST) * INV_ROOT
     place = lax.broadcasted_iota(jnp.int32, (1, positions), 1)
@@ -125,55 +126,47 @@
         stats = jnp.zeros((nodes, LANES), jnp.float32)
         for head in range(heads_here):
             at = (block * heads_here + head) * nodes
-            out_ref[block, head, 0] = summed[at : at + nodes]
+            out_refs[block][head, 0] = summed[at : at + nodes]
             stats = jnp.where(lane == head, top[at : at + nodes], stats)
             stats = jnp.where(lane == heads_here + head, high[at : at + nodes], stats)
             stats = jnp.where(lane == 2 * heads_here + head, low[at : at + nodes], stats)
-        out_ref[block, heads_here, 0] = stats.astype(jnp.bfloat16)
-
-
-def attend(meta, every_query, keys, values):
-    column_count, requests, nodes, width_here = every_query.shape
+        out_refs[block][heads_here, 0] = stats.astype(jnp.bfloat16)
+
+
+def attend(meta, queries, keys, values):
+    blocks = len(queries)
+    requests, nodes, width_here = queries[0].shape
     heads_here = width_here // HEAD_WIDTH
-    kv_heads = keys.shape[2] // HEAD_WIDTH
-    blocks = column_count // kv_heads
     prefix_here = keys.shape[1]
-
-    def query_spec(block):
-        def index(r, g, m):
-            return (m[requests] - (g * blocks + block) + column_count) % column_count, r, 0, 0
-
-        return pl.BlockSpec((1, 1, nodes, width_here), index)
-
+    out_block = (heads_here + 1, requests, nodes, HEAD_WIDTH)
+    cache_spec = pl.BlockSpec((1, prefix_here, HEAD_WIDTH), lambda r, m: (r, 0, m[requests]))
     return pl.pallas_call(
         functools.partial(attend_kernel, blocks),
         grid_spec=pltpu.PrefetchScalarGridSpec(
             num_scalar_prefetch=1,
-            grid=(requests, kv_heads),
-            in_specs=[
-                *[query_spec(block) for block in range(blocks)],
-                pl.BlockSpec((1, prefix_here, HEAD_WIDTH), lambda r, g, m: (r, 0, g)),
-                pl.BlockSpec((1, prefix_here, HEAD_WIDTH), lambda r, g, m: (r, 0, g)),
-            ],
-            out_specs=pl.BlockSpec(
-                (blocks, heads_here + 1, 1, nodes, HEAD_WIDTH), lambda r, g, m: (g, 0, r, 0, 0)
-            ),
-        ),
-        out_shape=jax.ShapeDtypeStruct(
-            (column_count, heads_here + 1, requests, nodes, HEAD_WIDTH), jnp.bfloat16
-        ),
+            grid=(requests,),
+            in_specs=[pl.BlockSpec((1, nodes, width_here), lambda r, m: (r, 0, 0))] * blocks
+            + [cache_spec, cache_spec],
+            out_specs=[
+                pl.BlockSpec((heads_here + 1, 1, nodes, HEAD_WIDTH), lambda r, m: (0, r, 0, 0))
+            ]
+            * blocks,
+        ),
+        out_shape=[jax.ShapeDtypeStruct(out_block, jnp.bfloat16)] * blocks,
         compiler_params=params(),
         cost_estimate=pl.CostEstimate(
-            flops=4 * requests * nodes * width_here * column_count * prefix_here,
-            bytes_accessed=4 * requests * prefix_here * kv_heads * HEAD_WIDTH,
-            transcendentals=requests * nodes * heads_here * column_count * prefix_here,
+            flops=4 * requests * nodes * width_here * blocks * prefix_here,
+            bytes_accessed=4 * requests * prefix_here * HEAD_WIDTH,
+            transcendentals=requests * nodes * heads_here * blocks * prefix_here,
         ),
         name="attend",
-    )(meta, *[every_query] * blocks, keys, values)
-
-
-def merge_kernel(kv_ref, got_ref, q_ref, tk_ref, tv_ref, linked_ref, out_ref):
-    sources, more, _, nodes, _ = got_ref.shape
+    )(meta, *queries, keys, values)
+
+
+def merge_kernel(kv_ref, q_ref, tk_ref, tv_ref, linked_ref, *refs):
+    got_refs, out_ref = refs[:-1], refs[-1]
+    sources = len(got_refs)
+    more, _, nodes, _ = got_refs[0].shape
     heads = more - 1
     query = jnp.concatenate(
         [q_ref[0, :, h * HEAD_WIDTH : (h + 1) * HEAD_WIDTH] for h in range(heads)], axis=0
@@ -183,7 +176,7 @@
     top = jnp.max(jnp.where(linked, scores, NEG_FILL), axis=1, keepdims=True)
     tops, totals = [], []
     for source in range(sources):
-        stats = got_ref[source, heads, 0].astype(jnp.float32)
+        stats = got_refs[source][heads, 0].astype(jnp.float32)
 
         def columns(first):
             return jnp.concatenate([stats[:, first + h : first + h + 1] for h in range(heads)], axis=0)
@@ -198,7 +191,7 @@
     for source in range(sources):
         factor = jnp.exp(tops[source] - top)
         total = total + totals[source] * factor
-        part = jnp.concatenate([got_ref[source, h, 0] for h in range(heads)], axis=0)
+        part = jnp.concatenate([got_refs[source][h, 0] for h in range(heads)], axis=0)
         summed = summed + part.astype(jnp.float32) * factor
     attended = (summed / total).astype(jnp.bfloat16)
     for h in range(heads):
@@ -206,7 +199,7 @@
 
 
 def merge(kv_group, got, queries, tree_keys, tree_values, linked):
-    sources, more, requests, nodes, _ = got.shape
+    more, requests, nodes, _ = got[0].shape
     width_here = queries.shape[2]
     return pl.pallas_call(
         merge_kernel,
@@ -214,18 +207,18 @@
             num_scalar_prefetch=1,
             grid=(requests,),
             in_specs=[
-                pl.BlockSpec((sources, more, 1, nodes, HEAD_WIDTH), lambda r, k: (0, 0, r, 0, 0)),
                 pl.BlockSpec((1, nodes, width_here), lambda r, k: (r, 0, 0)),
                 pl.BlockSpec((1, nodes, HEAD_WIDTH), lambda r, k: (r, 0, k[0])),
                 pl.BlockSpec((1, nodes, HEAD_WIDTH), lambda r, k: (r, 0, k[0])),
                 pl.BlockSpec((1, nodes, nodes), lambda r, k: (r, 0, 0)),
-            ],
+            ]
+            + [pl.BlockSpec((more, 1, nodes, HEAD_WIDTH), lambda r, k: (0, r, 0, 0))] * len(got),
             out_specs=pl.BlockSpec((1, nodes, width_here), lambda r, k: (r, 0, 0)),
         ),
         out_shape=jax.ShapeDtypeStruct((requests, nodes, width_here), jnp.bfloat16),
         compiler_params=params(),
         name="merge",
-    )(kv_group, got, queries, tree_keys, tree_values, linked)
+    )(kv_group, queries, tree_keys, tree_values, linked, *got)
 
 
 def project_kernel(slot_ref, x_ref, down_ref, w_ref, out_ref):
@@ -323,10 +316,8 @@
     requests, nodes, width_here = queries.shape
     columns = lax.axis_size("mp")
     column = lax.axis_index("mp")
-    heads_here = width_here // HEAD_WIDTH
     prefix_here = prefix_key_cache.shape[1]
     kv_heads = prefix_key_cache.shape[2] // HEAD_WIDTH
-    group_size = heads_here * columns // kv_heads
     batch_size = lax.axis_size("batch")
     batch_row = lax.axis_index("batch")
     present, rank, _ = adapter_down_weight.shape
@@ -353,11 +344,27 @@
     distance = (batch_row - my_owner + batch_size) % batch_size
     slot_code = distance * CAP + jnp.sum(earlier.astype(jnp.int32), axis=1)
 
-    every_query = jnp.stack(exchange([queries] * columns, "mp"), axis=0)
-    meta = jnp.concatenate([left, column.reshape(1)])
-    partial = attend(meta, every_query, prefix_key_cache, prefix_value_cache)
-    got = lax.all_to_all(partial, "mp", split_axis=0, concat_axis=0, tiled=True)
-    kv_group = (column * heads_here // group_size).reshape(1)
+    peers = columns // kv_heads
+    own_group = column // peers
+
+    def step(block, j, e):
+        if j == 0 and e % peers == 0:
+            return block
+        pairs = [
+            (i, (i // peers + j) % kv_heads * peers + (i % peers + e) % peers)
+            for i in range(columns)
+        ]
+        return lax.ppermute(block, "mp", pairs)
+
+    group_queries = [
+        [step(queries, -j, -e) for e in range(peers)] for j in range(kv_heads)
+    ]
+    got = []
+    for j in range(kv_heads):
+        meta = jnp.concatenate([left, ((own_group + j) % kv_heads).reshape(1)])
+        partial = attend(meta, group_queries[j], prefix_key_cache, prefix_value_cache)
+        got.extend(step(partial[e], j, e) for e in range(peers))
+    kv_group = own_group.reshape(1)
     attended = merge(
         kv_group, got, queries, tree_node_keys, tree_node_values, ancestors(parents)
     )

time: 115 us -> 113 us (0.983)
  the two profiles are of different devices: /device:TPU:27 before, /device:TPU:0 now
where the time goes in v4:
time: 113 us; the launch traced here: 112 us
  Pallas kernels  42.8 us (38%)
  starting transfers between devices  32.8 us (29%)
  waiting for transfers between devices  22 us (19%)
  local copies, waits for them, and re-layouts  11.3 us (10%)
  other arithmetic  2.56 us (2%)
    ppermute x9, starting transfers between devices, exchange(): got.append(lax.ppermute(blocks[shift], axis, pairs))  27.5 us
    pallas_call x4, Pallas kernels, attend(): pl.pallas_call(functools.partial(attend_kernel, blocks), grid_spec=pltpu....  19.5 us
    ppermute x9, waiting for transfers between devices, exchange(): got.append(lax.ppermute(blocks[shift], axis, pairs))  18.9 us
    pallas_call x4, Pallas kernels, project(): pl.pallas_call(project_kernel, grid_spec=pltpu.PrefetchScalarGridSpec(num...  14.6 us
    unnamed x41, local copies, waits for them, and re-layouts  10.3 us
    ppermute x6, starting transfers between devices, step(): return lax.ppermute(block, 'mp', pairs)  5.24 us
    pallas_call x1, Pallas kernels, merge(): pl.pallas_call(merge_kernel, grid_spec=pltpu.PrefetchScalarGridSpec(num_s...  3.84 us
    ppermute x6, waiting for transfers between devices, step(): return lax.ppermute(block, 'mp', pairs)  3.1 us
  transfers between devices with their start and end apart: 15, of which 3 were waited for; matrix products, arithmetic and copies ran while one was open for 6% of the time, Pallas kernels for 36%

profile of v4, /device:TPU:0, one launch (start us, length us, event | category | flops | bytes accessed | tf_op | source)
XLA Modules:
  0.0 112.4 jit_solution(9471360358557593401)
XLA Ops:
  0.0 2.4 %collective-permute-start.6 = (bf16[4,32,1024]{2,1,0:T(8,128)(2,1)}, bf16[4,32,1024]{2,1,0:T(8,128)(2,1)}, u32[]{:S(2)}, u32[]{:S(2)}) collective-permute-start(bf16[4,32,1024]{2,1,0:T(8,128)(2,1)} %q_ref.1), channel_id=1, source_target_pairs={{0,3},{1,0},{2,1},{3,2},{4,7},{5,4},{6,5},{7,6},{8,11},{9,8},{10,9... | collective-permute-start | bytes 786440 | tf_op jit(solution)/shard_map/ppermute | solution.py:357
  2.4 0.6 collective-permute-start.8
  3.0 0.2 collective-permute-start.10
  3.2 0.7 reshape.168
  4.0 0.2 reduce_window_sum.11
  4.2 0.1 select_reduce_fusion.1
  4.4 0.2 select_reduce_fusion
  4.7 0.7 broadcast_subtract_fusion.left_ref
  5.4 1.2 %copy-done.3 = bf16[4,64,2048]{2,1,0:T(8,128)(2,1)S(1)} copy-done((bf16[4,64,2048]{2,1,0:T(8,128)(2,1)S(1)}, bf16[4,64,2048]{2,1,0:T(8,128)(2,1)}, u32[]{:S(2)}) %copy-start.3) | copy-done | bytes 1048600
  6.6 1.0 copy-done.4
  7.6 2.4 %pick.1 = (s32[4]{0:T(128)S(1)}, bf16[2,64,2048]{2,1,0:T(8,128)(2,1)S(1)}, bf16[2,64,2048]{2,1,0:T(8,128)(2,1)}, bf16[2,64,2048]{2,1,0:T(8,128)(2,1)}, bf16[2,64...) custom-call(s32[8]{0:T(128)S(1)} %reshape.169.picked_ref, ...), custom_call_target="tpu_custom_call" | custom-call | tf_op jit(solution)/shard_map/pick/pallas_call | solution.py:77
  10.1 0.7 copy-done.5
  10.8 0.8 copy-done.9
  11.6 0.7 copy-done.11
  12.3 0.7 copy-done.13
  13.0 0.7 copy-done.15
  13.7 1.6 %collective-permute-start = (bf16[2,64,2048]{2,1,0:T(8,128)(2,1)}, bf16[2,64,2048]{2,1,0:T(8,128)(2,1)}, u32[]{:S(2)}, u32[]{:S(2)}) collective-permute-start(bf16[2,64,2048]{2,1,0:T(8,128)(2,1)} %get-tuple-element.15), channel_id=1, source_target_pairs={{0,4},{4,8},{8,12},{12,0},{1,5},{5,9},{9,13},{13,1},{2,6},{6,10},{... | collective-permute-start | bytes 1572872 | tf_op jit(solution)/shard_map/ppermute | solution.py:96
  15.3 2.6 %collective-permute-start.1 = (bf16[2,64,2048]{2,1,0:T(8,128)(2,1)}, bf16[2,64,2048]{2,1,0:T(8,128)(2,1)}, u32[]{:S(2)}, u32[]{:S(2)}) collective-permute-start(bf16[2,64,2048]{2,1,0:T(8,128)(2,1)} %get-tuple-element.16), channel_id=1, source_target_pairs={{0,8},{4,12},{8,0},{12,4},{1,9},{5,13},{9,1},{13,5},{2,10},{6,14},... | collective-permute-start | bytes 1572872 | tf_op jit(solution)/shard_map/ppermute | solution.py:96
  17.9 0.7 and_select_fusion.2
  18.7 0.2 convert_reduce_fusion
  18.9 0.4 fusion.1
  19.3 0.3 fusion.3
  19.9 2.2 %copy-done = bf16[4,1024,512]{2,1,0:T(8,128)(2,1)S(1)} copy-done((bf16[4,1024,512]{2,1,0:T(8,128)(2,1)S(1)}, bf16[4,1024,512]{2,1,0:T(8,128)(2,1)}, u32[]{:S(2)}) %copy-start) | copy-done | bytes 4194328
  22.1 5.1 %attend.4.refs_0_ = bf16[9,4,32,128]{3,2,1,0:T(8,128)(2,1)S(1)} custom-call(s32[5]{0:T(128)S(1)} %get-tuple-element.32.meta_ref, bf16[4,32,1024]{2,1,0:T(8,128)(2,1)S(1)} %copy-done.2, bf16[4,1024,512]{2,1,0:T(8,128)(2,1)S(1)} %copy-done, bf16[4,1024,512]{2,1,0:T(8,128)(2,1)} %refs_2_.7), custom_call_target="tpu_custom_call" | custom-call | flops 536870912 | bytes 2097152 | tf_op jit(solution)/shard_map/attend/pallas_call | solution.py:143
  27.3 1.4 %collective-permute-start.2 = (bf16[2,64,2048]{2,1,0:T(8,128)(2,1)S(1)}, bf16[2,64,2048]{2,1,0:T(8,128)(2,1)S(1)}, u32[]{:S(2)}, u32[]{:S(2)}) collective-permute-start(bf16[2,64,2048]{2,1,0:T(8,128)(2,1)S(1)} %copy-done.10), channel_id=1, source_target_pairs={{0,12},{4,0},{8,4},{12,8},{1,13},{5,1},{9,5},{13,9},{2,14},{6,2},{... | collective-permute-start | bytes 1572872 | tf_op jit(solution)/shard_map/ppermute | solution.py:96
  28.7 4.8 %attend.5 = bf16[9,4,32,128]{3,2,1,0:T(8,128)(2,1)S(1)} custom-call(s32[5]{0:T(128)S(1)} %get-tuple-element.30.meta_ref, bf16[4,32,1024]{2,1,0:T(8,128)(2,1)} %collective-permute-done.6.refs_0_, bf16[4,1024,512]{2,1,0:T(8,128)(2,1)S(1)} %copy-done.1, bf16[4,1024,512]{2,1,0:T(8,128)(2,1)} %refs_2_.7), custom_call_target="tpu_custom_call" | custom-call | flops 536870912 | bytes 2097152 | tf_op jit(solution)/shard_map/attend/pallas_call | solution.py:143
  33.5 0.5 collective-permute-start.5
  34.0 4.8 %attend.6 = bf16[9,4,32,128]{3,2,1,0:T(8,128)(2,1)S(1)} custom-call(s32[5]{0:T(128)S(1)} %get-tuple-element.31.meta_ref, bf16[4,32,1024]{2,1,0:T(8,128)(2,1)S(1)} %collective-permute-done.8.refs_0_, bf16[4,1024,512]{2,1,0:T(8,128)(2,1)S(1)} %copy-done.1, bf16[4,1024,512]{2,1,0:T(8,128)(2,1)} %refs_2_.7), custom_call_target="tpu_custom_call" | custom-call | flops 536870912 | bytes 2097152 | tf_op jit(solution)/shard_map/attend/pallas_call | solution.py:143
  38.8 0.3 collective-permute-start.7
  39.1 4.8 %attend.7 = bf16[9,4,32,128]{3,2,1,0:T(8,128)(2,1)S(1)} custom-call(s32[5]{0:T(128)S(1)} %get-tuple-element.29.meta_ref, bf16[4,32,1024]{2,1,0:T(8,128)(2,1)S(1)} %collective-permute-done.10.refs_0_, bf16[4,1024,512]{2,1,0:T(8,128)(2,1)S(1)} %copy-done.1, bf16[4,1024,512]{2,1,0:T(8,128)(2,1)} %refs_2_.7), custom_call_target="tpu_custom_call" | custom-call | flops 536870912 | bytes 2097152 | tf_op jit(solution)/shard_map/attend/pallas_call | solution.py:143
  43.9 1.1 collective-permute-start.9
  45.0 1.1 constant_dynamic-update-slice_fusion.2
  46.1 7.1 %collective-permute-done.1 = bf16[2,64,2048]{2,1,0:T(8,128)(2,1)} collective-permute-done((bf16[2,64,2048]{2,1,0:T(8,128)(2,1)}, bf16[2,64,2048]{2,1,0:T(8,128)(2,1)}, u32[]{:S(2)}, u32[]{:S(2)}) %collective-permute-start.1) | collective-permute-done | bytes 524320 | tf_op jit(solution)/shard_map/ppermute | solution.py:96
  53.2 0.7 collective-permute-start.11
  53.9 1.1 constant_dynamic-update-slice_fusion.1
  55.1 3.1 %collective-permute-done.11.refs_3_ = bf16[9,4,32,128]{3,2,1,0:T(8,128)(2,1)S(1)} collective-permute-done((bf16[9,4,32,128]{3,2,1,0:T(8,128)(2,1)S(1)}, bf16[9,4,32,128]{3,2,1,0:T(8,128)(2,1)S(1)}, u32[]{:S(2)}, u32[]{:S(2)}) %collective-permute-start.11) | collective-permute-done | bytes 294944 | tf_op jit(solution)/shard_map/ppermute | solution.py:357
  58.2 3.8 %merge.1.x_ref = bf16[4,32,1024]{2,1,0:T(8,128)(2,1)S(1)} custom-call(s32[1]{0:T(128)} %bitcast.1.kv_ref, bf16[4,32,1024]{2,1,0:T(8,128)(2,1)S(1)} %copy-done.2, bf16[4,32,512]{2,1,0:T(8,128)(2,1)S(1)} %copy-done.7, bf16[4,32,512]{2,1,0:T(8,128)(2,1)S(1)} %copy-done.8, f32[4,32,32]{2,1,0:T(8,128)S(1)} %convolution_minimum_fusion.linked_ref, ...), custom_call_target="tpu_custom_call" | custom-call | tf_op jit(solution)/shard_map/merge/pallas_call | solution.py:204
  62.0 3.6 %project.5 = bf16[128,2176]{1,0:T(8,128)(2,1)S(1)} custom-call(s32[5]{0:T(128)S(1)} %get-tuple-element.26.slot_ref, bf16[4,32,1024]{2,1,0:T(8,128)(2,1)S(1)} %merge.1.x_ref, bf16[8,64,2048]{2,1,0:T(8,128)(2,1)S(1)} %constant_dynamic-update-slice_fusion.down_ref.first_ref, bf16[1024,8192]{1,0:T(8,128)(2,1)} %w_ref.7), custom_call_target="tpu_custom_call" | custom-call | flops 536870912 | bytes 4194304 | tf_op jit(solution)/shard_map/project/pallas_call | solution.py:241
  65.6 1.3 %collective-permute-start.12 = (bf16[128,2176]{1,0:T(8,128)(2,1)S(1)}, bf16[128,2176]{1,0:T(8,128)(2,1)S(1)}, u32[]{:S(2)}, u32[]{:S(2)}) collective-permute-start(bf16[128,2176]{1,0:T(8,128)(2,1)S(1)} %project.5), channel_id=1, source_target_pairs={{0,1},{1,2},{2,3},{3,0},{4,5},{5,6},{6,7},{7,4},{8,9},{9,10},{10,1... | collective-permute-start | bytes 1671176 | tf_op jit(solution)/shard_map/ppermute | solution.py:96
  66.9 3.6 %project.6 = bf16[128,2176]{1,0:T(8,128)(2,1)S(1)} custom-call(s32[5]{0:T(128)S(1)} %get-tuple-element.27.slot_ref, bf16[4,32,1024]{2,1,0:T(8,128)(2,1)S(1)} %merge.1.x_ref, bf16[8,64,2048]{2,1,0:T(8,128)(2,1)S(1)} %constant_dynamic-update-slice_fusion.down_ref.first_ref, bf16[1024,8192]{1,0:T(8,128)(2,1)} %w_ref.7), custom_call_target="tpu_custom_call" | custom-call | flops 536870912 | bytes 4194304 | tf_op jit(solution)/shard_map/project/pallas_call | solution.py:241
  70.6 1.0 collective-permute-start.13
  71.6 3.6 %project.7 = bf16[128,2176]{1,0:T(8,128)(2,1)S(1)} custom-call(s32[5]{0:T(128)S(1)} %get-tuple-element.25.slot_ref, bf16[4,32,1024]{2,1,0:T(8,128)(2,1)S(1)} %merge.1.x_ref, bf16[8,64,2048]{2,1,0:T(8,128)(2,1)S(1)} %constant_dynamic-update-slice_fusion.down_ref.first_ref, bf16[1024,8192]{1,0:T(8,128)(2,1)} %w_ref.7), custom_call_target="tpu_custom_call" | custom-call | flops 536870912 | bytes 4194304 | tf_op jit(solution)/shard_map/project/pallas_call | solution.py:241
  75.3 0.3 collective-permute-start.14
  75.6 12.1 %collective-permute-start.4 = (bf16[2,64,1024]{2,1,0:T(8,128)(2,1)S(1)}, bf16[2,64,1024]{2,1,0:T(8,128)(2,1)S(1)}, u32[]{:S(2)}, u32[]{:S(2)}) collective-permute-start(bf16[2,64,1024]{2,1,0:T(8,128)(2,1)S(1)} %copy-done.14), channel_id=1, source_target_pairs={{0,8},{4,12},{8,0},{12,4},{1,9},{5,13},{9,1},{13,5},{2,10},{6,14},... | collective-permute-start | bytes 786440 | tf_op jit(solution)/shard_map/ppermute | solution.py:96
  87.7 6.7 %collective-permute-start.3 = (bf16[2,64,1024]{2,1,0:T(8,128)(2,1)S(1)}, bf16[2,64,1024]{2,1,0:T(8,128)(2,1)S(1)}, u32[]{:S(2)}, u32[]{:S(2)}) collective-permute-start(bf16[2,64,1024]{2,1,0:T(8,128)(2,1)S(1)} %copy-done.12), channel_id=1, source_target_pairs={{0,4},{4,8},{8,12},{12,0},{1,5},{5,9},{9,13},{13,1},{2,6},{6,10},{... | collective-permute-start | bytes 786440 | tf_op jit(solution)/shard_map/ppermute | solution.py:96
  94.4 11.7 %collective-permute-done.3 = bf16[2,64,1024]{2,1,0:T(8,128)(2,1)S(1)} collective-permute-done((bf16[2,64,1024]{2,1,0:T(8,128)(2,1)S(1)}, bf16[2,64,1024]{2,1,0:T(8,128)(2,1)S(1)}, u32[]{:S(2)}, u32[]{:S(2)}) %collective-permute-start.3) | collective-permute-done | bytes 262176 | tf_op jit(solution)/shard_map/ppermute | solution.py:96
  106.3 3.6 %project.4.refs_0_ = bf16[128,2176]{1,0:T(8,128)(2,1)S(1)} custom-call(s32[5]{0:T(128)S(1)} %get-tuple-element.28.slot_ref, bf16[4,32,1024]{2,1,0:T(8,128)(2,1)S(1)} %merge.1.x_ref, bf16[8,64,2048]{2,1,0:T(8,128)(2,1)S(1)} %constant_dynamic-update-slice_fusion.down_ref.first_ref, bf16[1024,8192]{1,0:T(8,128)(2,1)} %w_ref.7), custom_call_target="tpu_custom_call" | custom-call | flops 536870912 | bytes 4194304 | tf_op jit(solution)/shard_map/project/pallas_call | solution.py:241
  110.0 2.5 %finish.1 = bf16[4,32,2048]{2,1,0:T(8,128)(2,1)} custom-call(s32[4]{0:T(128)S(1)} %fusion.17.slot_ref, bf16[8,64,2048]{2,1,0:T(8,128)(2,1)S(1)} %constant_dynamic-update-slice_fusion.down_ref.first_ref, bf16[8,64,1024]{2,1,0:T(8,128)(2,1)S(1)} %pad_maximum_fusion.second_ref, bf16[128,2176]{1,0:T(8,128)(2,1)S(1)} %project.4.refs_0_, ...), custom_call_target="tpu_custom_call" | custom-call | tf_op jit(solution)/shard_map/finish/pallas_call | solution.py:289
  (56 shorter events, 1.0 us)
Async XLA Ops:
  0.0 19.9 %copy-start.2 = (bf16[4,32,1024]{2,1,0:T(8,128)(2,1)S(1)}, bf16[4,32,1024]{2,1,0:T(8,128)(2,1)}, u32[]{:S(2)}) copy-start(bf16[4,32,1024]{2,1,0:T(8,128)(2,1)} %q_ref.1) | copy-start | bytes 786436
  0.0 27.3 %collective-permute-start.6 = (bf16[4,32,1024]{2,1,0:T(8,128)(2,1)}, bf16[4,32,1024]{2,1,0:T(8,128)(2,1)}, u32[]{:S(2)}, u32[]{:S(2)}) collective-permute-start(bf16[4,32,1024]{2,1,0:T(8,128)(2,1)} %q_ref.1), channel_id=1, source_target_pairs={{0,3},{1,0},{2,1},{3,2},{4,7},{5,4},{6,5},{7,6},{8,11},{9,8},{10,9... | collective-permute-start | bytes 786440 | tf_op jit(solution)/shard_map/ppermute | solution.py:357
  2.4 31.1 %collective-permute-start.8 = (bf16[4,32,1024]{2,1,0:T(8,128)(2,1)}, bf16[4,32,1024]{2,1,0:T(8,128)(2,1)S(1)}, u32[]{:S(2)}, u32[]{:S(2)}) collective-permute-start(bf16[4,32,1024]{2,1,0:T(8,128)(2,1)} %q_ref.1), channel_id=1, source_target_pairs={{0,2},{1,3},{2,0},{3,1},{4,6},{5,7},{6,4},{7,5},{8,10},{9,11},{10,... | collective-permute-start | bytes 786440 | tf_op jit(solution)/shard_map/ppermute | solution.py:357
  3.0 35.8 %collective-permute-start.10 = (bf16[4,32,1024]{2,1,0:T(8,128)(2,1)}, bf16[4,32,1024]{2,1,0:T(8,128)(2,1)S(1)}, u32[]{:S(2)}, u32[]{:S(2)}) collective-permute-start(bf16[4,32,1024]{2,1,0:T(8,128)(2,1)} %q_ref.1), channel_id=1, source_target_pairs={{0,1},{1,2},{2,3},{3,0},{4,5},{5,6},{6,7},{7,4},{8,9},{9,10},{10,1... | collective-permute-start | bytes 786440 | tf_op jit(solution)/shard_map/ppermute | solution.py:357
  5.4 1.2 %copy-start.3 = (bf16[4,64,2048]{2,1,0:T(8,128)(2,1)S(1)}, bf16[4,64,2048]{2,1,0:T(8,128)(2,1)}, u32[]{:S(2)}) copy-start(bf16[4,64,2048]{2,1,0:T(8,128)(2,1)} %up_ref.1) | copy-start | bytes 3145732
  6.6 1.0 copy-start.4
  7.6 11.2 %copy-start.18 = (s32[4,32]{1,0:T(4,128)S(1)}, s32[4,32]{1,0:T(4,128)}, u32[]{:S(2)}) copy-start(s32[4,32]{1,0:T(4,128)} %param.17) | copy-start | bytes 1540
  7.6 12.0 %copy-start.17 = (s32[16]{0:T(128)S(1)}, s32[16]{0:T(128)}, u32[]{:S(2)}) copy-start(s32[16]{0:T(128)} %param.18) | copy-start | bytes 196
  10.1 0.7 copy-start.5
  10.8 0.8 copy-start.9
  11.6 0.7 copy-start.11
  12.3 0.7 copy-start.13
  13.0 0.7 copy-start.15
  13.7 30.2 %collective-permute-start = (bf16[2,64,2048]{2,1,0:T(8,128)(2,1)}, bf16[2,64,2048]{2,1,0:T(8,128)(2,1)}, u32[]{:S(2)}, u32[]{:S(2)}) collective-permute-start(bf16[2,64,2048]{2,1,0:T(8,128)(2,1)} %get-tuple-element.15), channel_id=1, source_target_pairs={{0,4},{4,8},{8,12},{12,0},{1,5},{5,9},{9,13},{13,1},{2,6},{6,10},{... | collective-permute-start | bytes 1572872 | tf_op jit(solution)/shard_map/ppermute | solution.py:96
  15.3 37.9 %collective-permute-start.1 = (bf16[2,64,2048]{2,1,0:T(8,128)(2,1)}, bf16[2,64,2048]{2,1,0:T(8,128)(2,1)}, u32[]{:S(2)}, u32[]{:S(2)}) collective-permute-start(bf16[2,64,2048]{2,1,0:T(8,128)(2,1)} %get-tuple-element.16), channel_id=1, source_target_pairs={{0,8},{4,12},{8,0},{12,4},{1,9},{5,13},{9,1},{13,5},{2,10},{6,14},... | collective-permute-start | bytes 1572872 | tf_op jit(solution)/shard_map/ppermute | solution.py:96
  19.9 2.2 %copy-start = (bf16[4,1024,512]{2,1,0:T(8,128)(2,1)S(1)}, bf16[4,1024,512]{2,1,0:T(8,128)(2,1)}, u32[]{:S(2)}) copy-start(bf16[4,1024,512]{2,1,0:T(8,128)(2,1)} %refs_1_.7) | copy-start | bytes 12582916
  22.1 5.2 %copy-start.10 = (bf16[2,64,2048]{2,1,0:T(8,128)(2,1)S(1)}, bf16[2,64,2048]{2,1,0:T(8,128)(2,1)}, u32[]{:S(2)}) copy-start(bf16[2,64,2048]{2,1,0:T(8,128)(2,1)} %copy-done.9) | copy-start | bytes 1572868
  22.1 6.6 %copy-start.1 = (bf16[4,1024,512]{2,1,0:T(8,128)(2,1)S(1)}, bf16[4,1024,512]{2,1,0:T(8,128)(2,1)}, u32[]{:S(2)}) copy-start(bf16[4,1024,512]{2,1,0:T(8,128)(2,1)} %refs_1_.7) | copy-start | bytes 12582916
  27.3 27.7 %collective-permute-start.2 = (bf16[2,64,2048]{2,1,0:T(8,128)(2,1)S(1)}, bf16[2,64,2048]{2,1,0:T(8,128)(2,1)S(1)}, u32[]{:S(2)}, u32[]{:S(2)}) collective-permute-start(bf16[2,64,2048]{2,1,0:T(8,128)(2,1)S(1)} %copy-done.10), channel_id=1, source_target_pairs={{0,12},{4,0},{8,4},{12,8},{1,13},{5,1},{9,5},{13,9},{2,14},{6,2},{... | collective-permute-start | bytes 1572872 | tf_op jit(solution)/shard_map/ppermute | solution.py:96
  28.7 4.9 %copy-start.16 = (bf16[2,64,1024]{2,1,0:T(8,128)(2,1)S(1)}, bf16[2,64,1024]{2,1,0:T(8,128)(2,1)}, u32[]{:S(2)}) copy-start(bf16[2,64,1024]{2,1,0:T(8,128)(2,1)} %copy-done.15) | copy-start | bytes 786436
  33.5 54.2 %collective-permute-start.5 = (bf16[2,64,1024]{2,1,0:T(8,128)(2,1)S(1)}, bf16[2,64,1024]{2,1,0:T(8,128)(2,1)S(1)}, u32[]{:S(2)}, u32[]{:S(2)}) collective-permute-start(bf16[2,64,1024]{2,1,0:T(8,128)(2,1)S(1)} %copy-done.16), channel_id=1, source_target_pairs={{0,12},{4,0},{8,4},{12,8},{1,13},{5,1},{9,5},{13,9},{2,14},{6,2},{... | collective-permute-start | bytes 786440 | tf_op jit(solution)/shard_map/ppermute | solution.py:96
  38.8 16.2 %collective-permute-start.7 = (bf16[9,4,32,128]{3,2,1,0:T(8,128)(2,1)S(1)}, bf16[9,4,32,128]{3,2,1,0:T(8,128)(2,1)S(1)}, u32[]{:S(2)}, u32[]{:S(2)}) collective-permute-start(bf16[9,4,32,128]{3,2,1,0:T(8,128)(2,1)S(1)} %attend.5), channel_id=1, source_target_pairs={{0,1},{1,2},{2,3},{3,0},{4,5},{5,6},{6,7},{7,4},{8,9},{9,10},{10,1... | collective-permute-start | bytes 884744 | tf_op jit(solution)/shard_map/ppermute | solution.py:357
  43.9 14.2 %copy-start.7 = (bf16[4,32,512]{2,1,0:T(8,128)(2,1)S(1)}, bf16[4,32,512]{2,1,0:T(8,128)(2,1)}, u32[]{:S(2)}) copy-start(bf16[4,32,512]{2,1,0:T(8,128)(2,1)} %tk_ref.1) | copy-start | bytes 393220
  43.9 14.2 %copy-start.8 = (bf16[4,32,512]{2,1,0:T(8,128)(2,1)S(1)}, bf16[4,32,512]{2,1,0:T(8,128)(2,1)}, u32[]{:S(2)}) copy-start(bf16[4,32,512]{2,1,0:T(8,128)(2,1)} %tv_ref.1) | copy-start | bytes 393220
  43.9 11.1 %collective-permute-start.9 = (bf16[9,4,32,128]{3,2,1,0:T(8,128)(2,1)S(1)}, bf16[9,4,32,128]{3,2,1,0:T(8,128)(2,1)S(1)}, u32[]{:S(2)}, u32[]{:S(2)}) collective-permute-start(bf16[9,4,32,128]{3,2,1,0:T(8,128)(2,1)S(1)} %attend.6), channel_id=1, source_target_pairs={{0,2},{1,3},{2,0},{3,1},{4,6},{5,7},{6,4},{7,5},{8,10},{9,11},{10,... | collective-permute-start | bytes 884744 | tf_op jit(solution)/shard_map/ppermute | solution.py:357
  53.2 4.9 %collective-permute-start.11 = (bf16[9,4,32,128]{3,2,1,0:T(8,128)(2,1)S(1)}, bf16[9,4,32,128]{3,2,1,0:T(8,128)(2,1)S(1)}, u32[]{:S(2)}, u32[]{:S(2)}) collective-permute-start(bf16[9,4,32,128]{3,2,1,0:T(8,128)(2,1)S(1)} %attend.7), channel_id=1, source_target_pairs={{0,3},{1,0},{2,1},{3,2},{4,7},{5,4},{6,5},{7,6},{8,11},{9,8},{10,9... | collective-permute-start | bytes 884744 | tf_op jit(solution)/shard_map/ppermute | solution.py:357
  65.6 44.3 %collective-permute-start.12 = (bf16[128,2176]{1,0:T(8,128)(2,1)S(1)}, bf16[128,2176]{1,0:T(8,128)(2,1)S(1)}, u32[]{:S(2)}, u32[]{:S(2)}) collective-permute-start(bf16[128,2176]{1,0:T(8,128)(2,1)S(1)} %project.5), channel_id=1, source_target_pairs={{0,1},{1,2},{2,3},{3,0},{4,5},{5,6},{6,7},{7,4},{8,9},{9,10},{10,1... | collective-permute-start | bytes 1671176 | tf_op jit(solution)/shard_map/ppermute | solution.py:96
  70.6 39.4 %collective-permute-start.13 = (bf16[128,2176]{1,0:T(8,128)(2,1)S(1)}, bf16[128,2176]{1,0:T(8,128)(2,1)S(1)}, u32[]{:S(2)}, u32[]{:S(2)}) collective-permute-start(bf16[128,2176]{1,0:T(8,128)(2,1)S(1)} %project.6), channel_id=1, source_target_pairs={{0,2},{1,3},{2,0},{3,1},{4,6},{5,7},{6,4},{7,5},{8,10},{9,11},{10,... | collective-permute-start | bytes 1671176 | tf_op jit(solution)/shard_map/ppermute | solution.py:96
  71.6 4.0 %copy-start.14 = (bf16[2,64,1024]{2,1,0:T(8,128)(2,1)S(1)}, bf16[2,64,1024]{2,1,0:T(8,128)(2,1)}, u32[]{:S(2)}) copy-start(bf16[2,64,1024]{2,1,0:T(8,128)(2,1)} %copy-done.13) | copy-start | bytes 786436
  71.6 16.1 %copy-start.12 = (bf16[2,64,1024]{2,1,0:T(8,128)(2,1)S(1)}, bf16[2,64,1024]{2,1,0:T(8,128)(2,1)}, u32[]{:S(2)}) copy-start(bf16[2,64,1024]{2,1,0:T(8,128)(2,1)} %copy-done.11) | copy-start | bytes 786436
  71.6 34.5 %copy-start.6 = (bf16[2,64,1024]{2,1,0:T(8,128)(2,1)S(1)}, bf16[2,64,1024]{2,1,0:T(8,128)(2,1)}, u32[]{:S(2)}) copy-start(bf16[2,64,1024]{2,1,0:T(8,128)(2,1)} %copy-done.5) | copy-start | bytes 786436
  75.3 34.7 %collective-permute-start.14 = (bf16[128,2176]{1,0:T(8,128)(2,1)S(1)}, bf16[128,2176]{1,0:T(8,128)(2,1)S(1)}, u32[]{:S(2)}, u32[]{:S(2)}) collective-permute-start(bf16[128,2176]{1,0:T(8,128)(2,1)S(1)} %project.7), channel_id=1, source_target_pairs={{0,3},{1,0},{2,1},{3,2},{4,7},{5,4},{6,5},{7,6},{8,11},{9,8},{10,9... | collective-permute-start | bytes 1671176 | tf_op jit(solution)/shard_map/ppermute | solution.py:96
  75.6 18.8 %collective-permute-start.4 = (bf16[2,64,1024]{2,1,0:T(8,128)(2,1)S(1)}, bf16[2,64,1024]{2,1,0:T(8,128)(2,1)S(1)}, u32[]{:S(2)}, u32[]{:S(2)}) collective-permute-start(bf16[2,64,1024]{2,1,0:T(8,128)(2,1)S(1)} %copy-done.14), channel_id=1, source_target_pairs={{0,8},{4,12},{8,0},{12,4},{1,9},{5,13},{9,1},{13,5},{2,10},{6,14},... | collective-permute-start | bytes 786440 | tf_op jit(solution)/shard_map/ppermute | solution.py:96
  87.7 18.4 %collective-permute-start.3 = (bf16[2,64,1024]{2,1,0:T(8,128)(2,1)S(1)}, bf16[2,64,1024]{2,1,0:T(8,128)(2,1)S(1)}, u32[]{:S(2)}, u32[]{:S(2)}) collective-permute-start(bf16[2,64,1024]{2,1,0:T(8,128)(2,1)S(1)} %copy-done.12), channel_id=1, source_target_pairs={{0,4},{4,8},{8,12},{12,0},{1,5},{5,9},{9,13},{13,1},{2,6},{6,10},{... | collective-permute-start | bytes 786440 | tf_op jit(solution)/shard_map/ppermute | solution.py:96
